TPU v7x, 256 devices: a whole 4x4x8 slice. The times are simulated.
256 devices in a mesh: cells: 64 (over z_hi, y, x, core), tm: 4 (over z_lo).
Axes of the slice: x: 4, y: 4, z: 8 (z_hi: 2, z_lo: 4; z = z_hi * 4 + z_lo), core: 2. Of those that a mesh axis runs over, the one named last changes fastest.
Arguments:
- urban: float32 [2048, 8192], P('tm', 'cells')
- rural: float32 [2048, 8192], P('tm', 'cells')
- urban_valid: int32 [8192], P('cells'), may hold values from 1024 to 2048
- rural_ids: int32 [8, 8192], P(None, 'cells'), may hold values from 0 to 8191, as said below
Outputs:
- correlation: float32 [128, 8, 8192], P('tm', None, 'cells')
Inputs may be any that keep to these rules, and one draw needn't show every extreme that they name: `rural_ids`: the rural cell with id i lies on index i // 128 of cells. Of the 1024 references of the urban cells of one index of cells, at most 16 name rural cells of any one other index, and for every index some other index has exactly 16.
All inputs are finite; a program needn't handle non-finite values.
Results may differ from a plain program's by a relative error of at most 0.0024.
Values may be sent and summed in bfloat16 or wider, within the bound.
A program may use at most 128 MiB of HBM per device.

v0:
```python
import jax
import jax.numpy as jnp
from jax import lax
from jax.sharding import PartitionSpec as P

LAGS = 128


EPSILON = 1e-05


def shifted(x, axis, by):
    peers = lax.axis_size(axis)
    pairs = [(i, i + by) for i in range(peers) if 0 <= i + by < peers]
    return lax.ppermute(x, axis, pairs)


def finish(series, first_sum, second_sum, valid_count, valid_mask):
    average = first_sum / valid_count
    spread = second_sum / valid_count - average * average
    return ((series - average) * lax.rsqrt(spread + EPSILON) * valid_mask).astype(jnp.bfloat16)


def shards(urban, rural, urban_valid, rural_ids):
    hours_dev = urban.shape[0]
    cells_dev = urban.shape[1]
    rural_dev = rural.shape[1]
    refs_per = rural_ids.shape[0]
    lag_total = LAGS
    tm_count = lax.axis_size("tm")
    tm_index = lax.axis_index("tm")
    hour_idx = tm_index * hours_dev + jnp.arange(hours_dev, dtype=jnp.int32)
    urban_mask = (hour_idx[:, None] < urban_valid[None, :]).astype(jnp.float32)
    urban_one = jnp.sum(urban * urban_mask, axis=0)
    urban_two = jnp.sum(urban * urban * urban_mask, axis=0)
    rural_one = jnp.sum(rural, axis=0)
    rural_two = jnp.sum(rural * rural, axis=0)
    urban_one, urban_two, rural_one, rural_two = lax.psum(
        (urban_one, urban_two, rural_one, rural_two), "tm"
    )
    urban_z = finish(urban, urban_one, urban_two, urban_valid.astype(jnp.float32), urban_mask)
    rural_z = finish(
        rural,
        rural_one,
        rural_two,
        jnp.float32(hours_dev * tm_count),
        jnp.ones((1, 1), jnp.float32),
    )
    devices = lax.axis_size("cells")
    own_index = lax.axis_index("cells")
    capacity = cells_dev // 8
    flat_ids = rural_ids.reshape(-1)
    owners = flat_ids // rural_dev
    local_idx = flat_ids % rural_dev
    foreign = owners != own_index
    onehot = (owners[:, None] == jnp.arange(devices, dtype=jnp.int32)[None, :]) & foreign[:, None]
    slots_all = flat_ids.shape[0]
    slot_range = jnp.arange(slots_all, dtype=jnp.int32)
    lower = (slot_range[:, None] > slot_range[None, :]).astype(jnp.bfloat16)
    before = jnp.dot(lower, onehot.astype(jnp.bfloat16), preferred_element_type=jnp.float32)
    ranks = jnp.sum(jnp.where(onehot, before, 0.0), axis=1).astype(jnp.int32)
    slot_idx = jnp.where(foreign, owners * capacity + ranks, devices * capacity)
    requests = jnp.zeros((devices * capacity + 1,), jnp.int32).at[slot_idx].set(local_idx)
    requests = requests[: devices * capacity].reshape(devices, capacity)
    asked = lax.all_to_all(requests, "cells", split_axis=0, concat_axis=0, tiled=True)
    outgoing = rural_z[:, asked]
    fetched = lax.all_to_all(outgoing, "cells", split_axis=1, concat_axis=1, tiled=True)
    columns_all = jnp.concatenate([rural_z, fetched.reshape(hours_dev, devices * capacity)], 1)
    column_idx = jnp.where(foreign, rural_dev + slot_idx, local_idx)
    chosen = columns_all[:, column_idx].reshape(hours_dev, refs_per, cells_dev)
    empty = jnp.zeros((lag_total, refs_per, cells_dev), jnp.float32)
    previous = shifted(chosen[hours_dev - (lag_total - 1) :], "tm", 1)
    extended = jnp.concatenate([previous, chosen], 0)
    offsets = jnp.arange(lag_total, dtype=jnp.int32)
    back_idx = offsets[None, :] - offsets[:, None] + (lag_total - 1)

    def backward_step(block_idx, total):
        begin = block_idx * lag_total
        window = lax.dynamic_slice_in_dim(extended, begin, 2 * lag_total - 1, 0)
        toeplitz = window[back_idx]
        urban_block = lax.dynamic_slice_in_dim(urban_z, begin, lag_total, 0)
        return total + jnp.einsum(
            "sc,lskc->lkc", urban_block, toeplitz, preferred_element_type=jnp.float32
        )

    partial_sum = lax.fori_loop(0, hours_dev // lag_total, backward_step, empty)
    summed = lax.psum_scatter(partial_sum, "tm", scatter_dimension=0, tiled=True)
    lag_share = lag_total // tm_count
    lag_idx = tm_index * lag_share + jnp.arange(lag_share, dtype=jnp.int32)
    intersection = (urban_valid[None, None, :] - lag_idx[:, None, None]).astype(jnp.float32)
    return summed / intersection


def solution(mesh):
    in_specs = (P("tm", "cells"), P("tm", "cells"), P("cells"), P(None, "cells"))
    out_specs = P("tm", None, "cells")
    return jax.shard_map(shards, mesh=mesh, in_specs=in_specs, out_specs=out_specs, check_vma=False)
```

profile of v0, /device:TPU:1, one launch (start us, length us, event | category | flops | bytes accessed | tf_op | source)
XLA Modules:
  0.0 636.6 jit_solution(2759811206594511423)
XLA Ops:
  6.5 0.8 add_select_fusion
  7.3 0.7 broadcast_compare_fusion
  8.0 0.6 fusion.6
  8.6 0.7 compare_select_fusion.5
  9.4 4.3 scatter_custom_fusion
  13.7 0.7 all_to_all.11
  14.4 15.6 %all-to-all-start = ((s32[64,1,16]{2,1,0:T(1,128)}), s32[64,1,16]{2,1,0:T(1,128)S(1)}, u32[]{:S(2)}, u32[]{:S(2)}) async-start(s32[64,1,16]{2,1,0:T(1,128)} %bitcast.6), calls=%async_computation | async-start | bytes 65536 | tf_op jit(solution)/shard_map/all_to_all | solution.py:65
  30.0 1.0 fusion.19
  31.2 0.1 fusion.8
  31.4 8.9 %all-reduce = (f32[128]{0:T(128)S(1)}, f32[128]{0:T(128)S(1)}, f32[128]{0:T(128)S(1)}, f32[128]{0:T(128)S(1)}) all-reduce(f32[128]{0:T(128)S(1)} %get-tuple-element.120, f32[128]{0:T(128)S(1)} %get-tuple-element.119, f32[128]{0:T(128)S(1)} %get-tuple-element.118, f32[128]{0:T(128)S(1)} %get-tuple-element.117), channel_id=1, replica_groups=mesh['cells'=64,'tm'=4] {'tm'}, use_global_device_ids=true, to_apply=%region_3.0 | all-reduce | flops 512 | bytes 4096 | tf_op jit(solution)/shard_map/psum | solution.py:38
  40.4 1.3 all-to-all-done
  41.8 5.1 gather_fusion.1
  46.8 12.9 %all-to-all-start.1 = ((bf16[512,64,16]{0,2,1:T(8,128)(2,1)}), bf16[512,64,16]{0,2,1:T(8,128)(2,1)S(1)}, u32[]{:S(2)}, u32[]{:S(2)}) async-start(bf16[512,64,16]{0,2,1:T(8,128)(2,1)} %bitcast.9), calls=%async_computation.1 | async-start | bytes 2097152 | tf_op jit(solution)/shard_map/all_to_all | solution.py:67
  59.8 29.4 %all-to-all-done.1 = bf16[512,64,16]{0,2,1:T(8,128)(2,1)S(1)} async-done(((bf16[512,64,16]{0,2,1:T(8,128)(2,1)}), bf16[512,64,16]{0,2,1:T(8,128)(2,1)S(1)}, u32[]{:S(2)}, u32[]{:S(2)}) %all-to-all-start.1) | async-done | bytes 1048608 | tf_op jit(solution)/shard_map/all_to_all | solution.py:67
  89.4 4.0 gather_fusion.2
  93.5 0.2 copy.13
  93.7 4.0 collective-permute-start
  97.9 0.8 copy.14
  98.6 4.3 collective-permute-done
  103.0 503.0 %while.14 = (s32[]{:T(128)}, f32[128,8,128]{2,1,0:T(8,128)S(1)}, bf16[639,8,128]{2,1,0:T(8,128)(2,1)S(1)}, bf16[512,128]{1,0:T(8,128)(2,1)S(1)}, s32[]{:T(128)},...) while((s32[]{:T(128)}, f32[128,8,128]{2,1,0:T(8,128)S(1)}, ...), condition=%wide.region_11.12_spmd.clone, body=%wide.region_10.11_spmd.clone.sunk | while | flops 50577416 | bytes 104100016 | solution.py:86
  103.1 113.5 %gather_fusion = bf16[16384,8,128]{2,1,0:T(8,128)(2,1)} fusion(bf16[255,8,128]{2,1,0:T(8,128)(2,1)S(1)} %constant_dynamic-slice_fusion.2, s32[16384]{0:T(1024)S(1)} %fusion.21), kind=kCustom, calls=%fused_computation.clone.clone.1 | custom fusion | bytes 67174400 | tf_op jit(solution)/shard_map/while/body/eval_jaxpr/gather | solution.py:80
  216.6 12.0 %multiply_reduce_fusion.3 = f32[128,128,8]{0,2,1:T(8,128)S(1)} fusion(f32[128,128]{0,1:T(8,128)S(1)} %bitcast_convert_fusion.2, bf16[16384,8,128]{2,1,0:T(8,128)(2,1)} %gather_fusion), kind=kLoop, calls=%fused_computation.5.clone.1 | loop fusion | flops 50200576 | bytes 34144256 | tf_op jit(solution)/shard_map/while/body/eval_jaxpr/sc,lskc->lkc/dot_general | solution.py:82
  228.6 0.1 bitcast_add_fusion.2
  228.8 113.5 %gather_fusion = bf16[16384,8,128]{2,1,0:T(8,128)(2,1)} fusion(bf16[255,8,128]{2,1,0:T(8,128)(2,1)S(1)} %constant_dynamic-slice_fusion.2, s32[16384]{0:T(1024)S(1)} %fusion.21), kind=kCustom, calls=%fused_computation.clone.clone.1 | custom fusion | bytes 67174400 | tf_op jit(solution)/shard_map/while/body/eval_jaxpr/gather | solution.py:80
  342.3 12.0 %multiply_reduce_fusion.3 = f32[128,128,8]{0,2,1:T(8,128)S(1)} fusion(f32[128,128]{0,1:T(8,128)S(1)} %bitcast_convert_fusion.2, bf16[16384,8,128]{2,1,0:T(8,128)(2,1)} %gather_fusion), kind=kLoop, calls=%fused_computation.5.clone.1 | loop fusion | flops 50200576 | bytes 34144256 | tf_op jit(solution)/shard_map/while/body/eval_jaxpr/sc,lskc->lkc/dot_general | solution.py:82
  354.6 113.5 %gather_fusion = bf16[16384,8,128]{2,1,0:T(8,128)(2,1)} fusion(bf16[255,8,128]{2,1,0:T(8,128)(2,1)S(1)} %constant_dynamic-slice_fusion.2, s32[16384]{0:T(1024)S(1)} %fusion.21), kind=kCustom, calls=%fused_computation.clone.clone.1 | custom fusion | bytes 67174400 | tf_op jit(solution)/shard_map/while/body/eval_jaxpr/gather | solution.py:80
  468.1 12.0 %multiply_reduce_fusion.3 = f32[128,128,8]{0,2,1:T(8,128)S(1)} fusion(f32[128,128]{0,1:T(8,128)S(1)} %bitcast_convert_fusion.2, bf16[16384,8,128]{2,1,0:T(8,128)(2,1)} %gather_fusion), kind=kLoop, calls=%fused_computation.5.clone.1 | loop fusion | flops 50200576 | bytes 34144256 | tf_op jit(solution)/shard_map/while/body/eval_jaxpr/sc,lskc->lkc/dot_general | solution.py:82
  480.3 113.5 %gather_fusion = bf16[16384,8,128]{2,1,0:T(8,128)(2,1)} fusion(bf16[255,8,128]{2,1,0:T(8,128)(2,1)S(1)} %constant_dynamic-slice_fusion.2, s32[16384]{0:T(1024)S(1)} %fusion.21), kind=kCustom, calls=%fused_computation.clone.clone.1 | custom fusion | bytes 67174400 | tf_op jit(solution)/shard_map/while/body/eval_jaxpr/gather | solution.py:80
  593.8 12.0 %multiply_reduce_fusion.3 = f32[128,128,8]{0,2,1:T(8,128)S(1)} fusion(f32[128,128]{0,1:T(8,128)S(1)} %bitcast_convert_fusion.2, bf16[16384,8,128]{2,1,0:T(8,128)(2,1)} %gather_fusion), kind=kLoop, calls=%fused_computation.5.clone.1 | loop fusion | flops 50200576 | bytes 34144256 | tf_op jit(solution)/shard_map/while/body/eval_jaxpr/sc,lskc->lkc/dot_general | solution.py:82
  606.0 0.8 copy-done
  606.9 21.3 %reduce-scatter.2.cloned.1.call-done = f32[32,8,128]{2,1,0:T(8,128)} async-done(((f32[128,8,128]{2,1,0:T(8,128)}), f32[32,8,128]{2,1,0:T(8,128)}) %reduce-scatter.2.cloned.1.call-update) | async-done | bytes 131088 | tf_op jit(solution)/shard_map/reduce_scatter | solution.py:87
  628.2 1.6 broadcast_divide_fusion
  (42 shorter events, 1.6 us)
Async XLA Ops:
  6.5 24.5 %copy-start.1 = (f32[512,128]{1,0:T(8,128)S(1)}, f32[512,128]{1,0:T(8,128)}, u32[]{:S(2)}) copy-start(f32[512,128]{1,0:T(8,128)} %param.7) | copy-start | bytes 786436
  6.5 24.7 %copy-start.2 = (f32[512,128]{1,0:T(8,128)S(1)}, f32[512,128]{1,0:T(8,128)}, u32[]{:S(2)}) copy-start(f32[512,128]{1,0:T(8,128)} %param.6) | copy-start | bytes 786436
  6.5 24.7 %copy-start.3 = (s32[128]{0:T(128)S(1)}, s32[128]{0:T(128)}, u32[]{:S(2)}) copy-start(s32[128]{0:T(128)} %param.8) | copy-start | bytes 1540
  14.4 27.3 %all-to-all-start = ((s32[64,1,16]{2,1,0:T(1,128)}), s32[64,1,16]{2,1,0:T(1,128)S(1)}, u32[]{:S(2)}, u32[]{:S(2)}) async-start(s32[64,1,16]{2,1,0:T(1,128)} %bitcast.6), calls=%async_computation | async-start | bytes 65536 | tf_op jit(solution)/shard_map/all_to_all | solution.py:65
  46.8 42.4 %all-to-all-start.1 = ((bf16[512,64,16]{0,2,1:T(8,128)(2,1)}), bf16[512,64,16]{0,2,1:T(8,128)(2,1)S(1)}, u32[]{:S(2)}, u32[]{:S(2)}) async-start(bf16[512,64,16]{0,2,1:T(8,128)(2,1)} %bitcast.9), calls=%async_computation.1 | async-start | bytes 2097152 | tf_op jit(solution)/shard_map/all_to_all | solution.py:67
  59.8 568.4 %reduce-scatter.2.cloned.1.call-start = ((), (), s32[]{:S(2)}) async-start(), calls=%async_computation.3 | async-start | bytes 655360 | tf_op jit(solution)/shard_map/reduce_scatter | solution.py:87
  93.7 9.2 %collective-permute-start = (bf16[127,8,128]{2,1,0:T(8,128)(2,1)S(1)}, bf16[127,8,128]{2,1,0:T(8,128)(2,1)S(1)}, u32[]{:S(2)}, u32[]{:S(2)}) collective-permute-start(bf16[127,8,128]{2,1,0:T(8,128)(2,1)S(1)} %copy.13), channel_id=1, source_target_pairs={{0,1},{1,2},{2,3},{4,5},{5,6},{6,7},{8,9},{9,10},{10,11},{12,13},{... | collective-permute-start | bytes 780296 | tf_op jit(solution)/shard_map/ppermute | solution.py:15
  606.0 0.8 copy-start
Sparse Core Ops, SparseCore 0:
  606.9 21.2 reduce-scatter.1
where the time goes:
time: 638 us; the launch traced here: 637 us
  local copies, waits for them, and re-layouts  470 us (74%)
  waiting for transfers between devices  56.3 us (9%)
  other arithmetic  54.1 us (8%)
  starting transfers between devices  32.6 us (5%)
  between operations  13.6 us (2%)
  blocking collectives  8.88 us (1%)
    gather x4, local copies, waits for them, and re-layouts, backward_step(): toeplitz = window[back_idx]  454 us
    dot_general x4, other arithmetic, backward_step(): jnp.einsum('sc,lskc->lkc', urban_block, toeplitz, preferred_element_type=...  48 us
    all_to_all x1, waiting for transfers between devices, shards(): lax.all_to_all(outgoing, 'cells', split_axis=1, concat_axis=1, tiled=True)  29.4 us
    reduce_scatter x1, waiting for transfers between devices, shards(): lax.psum_scatter(partial_sum, 'tm', scatter_dimension=0, tiled=True)  21.3 us
    all_to_all x1, starting transfers between devices, shards(): lax.all_to_all(requests, 'cells', split_axis=0, concat_axis=0, tiled=True)  15.6 us
    all_to_all x1, starting transfers between devices, shards(): lax.all_to_all(outgoing, 'cells', split_axis=1, concat_axis=1, tiled=True)  12.9 us
  transfers between devices with their start and end apart: 4, of which 4 were waited for; matrix products, arithmetic and copies ran while one was open for 0% of the time, Pallas kernels for 0%

commit v1 on v0

v1 whole, which is shorter than its diff:
```python
import functools

import jax
import jax.numpy as jnp
from jax import lax
from jax.experimental import pallas as pl
from jax.experimental.pallas import tpu as pltpu
from jax.sharding import PartitionSpec as P

LAGS = 128
EPSILON = 1e-05
CAP = 16
GROUP = 32
MESH = pl.DeviceIdType.MESH
F32 = jnp.float32
BF16 = jnp.bfloat16

REQ, STAT, HALO, FETCH, PART = range(5)


def iota(shape, axis):
    return lax.broadcasted_iota(jnp.int32, shape, axis)


def bytes_wait(ref, sem):
    pltpu.make_async_copy(ref, ref, sem).wait()


def kernel(
    nc, nt, urban_ref, rural_ref, valid_ref, ids_ref, out_ref,
    req_out, req_in, req_acc, stats, ut, halo_out, halo_in, send, fetched, pick, toep, part, got, ssem, rsem,
):
    hours, cells = urban_ref.shape
    refs = ids_ref.shape[0]
    share = LAGS // nt
    groups = cells // GROUP
    wide = GROUP * refs
    slots = nc * CAP
    me = lax.axis_index("cells")
    tm = lax.axis_index("tm")

    def remote(kind, src, dst, **where):
        return pltpu.make_async_remote_copy(
            src_ref=src, dst_ref=dst, send_sem=ssem.at[kind], recv_sem=rsem.at[kind],
            device_id=where, device_id_type=MESH,
        )

    barrier = pltpu.get_barrier_semaphore()

    @pl.loop(1, nc)
    def _(d):
        pl.semaphore_signal(barrier, inc=1, device_id={"cells": lax.rem(me + d, nc)}, device_id_type=MESH)

    @pl.loop(1, nt)
    def _(d):
        pl.semaphore_signal(barrier, inc=1, device_id={"tm": lax.rem(tm + d, nt)}, device_id_type=MESH)

    valid = valid_ref[...].astype(F32)
    hour = (tm * hours + iota((hours, cells), 0)).astype(F32)
    mask = (hour < valid).astype(F32)
    urban = urban_ref[...]
    rural = rural_ref[...]
    mine = stats.at[tm]
    mine[0:1] = jnp.sum(urban * mask, axis=0, keepdims=True)
    mine[1:2] = jnp.sum(urban * urban * mask, axis=0, keepdims=True)
    mine[2:3] = jnp.sum(rural, axis=0, keepdims=True)
    mine[3:4] = jnp.sum(rural * rural, axis=0, keepdims=True)
    mine[4:8] = jnp.zeros((4, cells), F32)

    req_acc[...] = jnp.zeros_like(req_acc)
    ids = ids_ref[...]
    owners = (ids >> 7).astype(F32)
    lane = iota((GROUP, cells), 1)
    row = iota((GROUP, cells), 0)
    mef = me.astype(F32)

    @pl.loop(0, groups * refs)
    def _(block):
        g = block // refs
        k = block % refs
        one = (lane == GROUP * g + row)
        id_row = ids_ref[pl.ds(k, 1), :]
        owner = jnp.sum(jnp.where(one, (id_row >> 7).astype(F32), 0.0), axis=1, keepdims=True)
        local = jnp.sum(jnp.where(one, (id_row & 127).astype(F32), 0.0), axis=1, keepdims=True)
        place = k * cells + GROUP * g + row
        count = jnp.zeros((GROUP, cells), F32)
        for other in range(refs):
            earlier = (owners[other : other + 1] == owner) & (other * cells + lane < place)
            count += jnp.where(earlier, 1.0, 0.0)
        rank = jnp.sum(count, axis=1, keepdims=True)
        slot = jnp.where(owner == mef, slots + local, owner * CAP + rank).astype(jnp.int32)
        begin = pl.multiple_of(block * GROUP, GROUP)
        for j in range((slots + cells) // cells):
            hit = slot == lane + j * cells
            pick[pl.ds(begin, GROUP), j * cells : (j + 1) * cells] = jnp.where(hit, 1.0, 0.0).astype(BF16)
            if j < slots // cells:
                req_acc[:, j * cells : (j + 1) * cells] += jnp.where(hit, local, 0.0)

    asks = jnp.sum(req_acc[...], axis=0, keepdims=True).astype(jnp.int32)
    for j in range(slots // cells):
        req_out[j] = asks[:, j * cells : (j + 1) * cells]

    pl.semaphore_wait(barrier, nc - 1 + nt - 1)

    @pl.loop(1, nt)
    def _(d):
        remote(STAT, stats.at[tm], stats.at[tm], tm=lax.rem(tm + d, nt)).start()

    per = cells // CAP

    @pl.loop(1, nc)
    def _(d):
        peer = lax.rem(me + d, nc)
        remote(REQ, req_out.at[peer // per], req_in.at[me], cells=peer).start()

    req_in[me] = jnp.zeros((1, cells), jnp.int32)

    bytes_wait(stats.at[0 : nt - 1], rsem.at[STAT])
    total = stats[0]
    for i in range(1, nt):
        total += stats[i]

    def finish(series, first, second, n, keep):
        average = first / n
        spread = second / n - average * average
        return ((series - average) * lax.rsqrt(spread + EPSILON) * keep).astype(BF16).astype(F32)

    rural_z = finish(rural, total[2:3], total[3:4], F32(hours * nt), F32(1.0))
    rural_t = jnp.transpose(rural_z).astype(BF16)
    fetched[nc : nc + cells // CAP] = rural_t.reshape(cells // CAP, CAP, hours)
    urban_z = finish(urban, total[0:1], total[1:2], valid, mask)
    for j in range(hours // LAGS):
        ut[j] = jnp.transpose(urban_z[j * LAGS : (j + 1) * LAGS])
    halo_out[...] = ut[0].astype(BF16)

    @pl.when(tm > 0)
    def _():
        remote(HALO, halo_out, halo_in, tm=tm - 1).start()

    bytes_wait(req_in.at[0 : nc - 1], rsem.at[REQ])
    fetched[me] = jnp.zeros((CAP, hours), BF16)
    chunks = nc // per
    wanted = lax.rem(me, per) * CAP
    lane_c = iota((CAP, cells), 1)
    row_c = iota((CAP, cells), 0)
    here = lane_c == wanted + row_c

    @pl.loop(0, chunks)
    def _(step):
        q = lax.rem(me // per + step, chunks)
        columns = []
        for s in range(per):
            asked = req_in[q * per + s].astype(F32)
            columns.append(jnp.sum(jnp.where(here, asked, 0.0), axis=1, keepdims=True))
        column = jnp.concatenate(columns, axis=0).astype(jnp.int32)
        chosen = jnp.where(column == iota((cells, cells), 1), 1.0, 0.0).astype(BF16)
        rows = jnp.dot(chosen, fetched[nc : nc + cells // CAP].reshape(cells, hours), preferred_element_type=F32)
        send[pl.ds(q * per, per)] = rows.astype(BF16).reshape(per, CAP, hours)

        @pl.loop(0, per)
        def _(s):
            peer = q * per + s

            @pl.when(peer != me)
            def _():
                remote(FETCH, send.at[peer], fetched.at[me], cells=peer).start()

    @pl.when(tm < nt - 1)
    def _():
        bytes_wait(halo_in, rsem.at[HALO])
        ut[hours // LAGS] = halo_in[...].astype(F32)

    @pl.when(tm == nt - 1)
    def _():
        ut[hours // LAGS] = jnp.zeros((cells, LAGS), F32)

    tiles = hours // LAGS
    lane8 = iota((8, LAGS), 1)
    row8 = iota((8, LAGS), 0)

    @pl.loop(0, cells)
    def _(c):
        wave = [
            jnp.broadcast_to(ut[j, pl.ds(c, 1), :], (8, LAGS)) for j in range(tiles + 1)
        ]
        for pair in range(LAGS // 16):
            halves = []
            for a in (2 * pair, 2 * pair + 1):
                turned = [pltpu.roll(x, 8 * a + 1, 1, stride=1, stride_axis=0) for x in wave]
                upper = lane8 >= row8 + (8 * a + 1)
                halves.append([jnp.where(upper, turned[j + 1], turned[j]) for j in range(tiles)])
            for j in range(tiles):
                both = jnp.concatenate([halves[0][j], halves[1][j]], axis=0).astype(BF16)
                toep[c, 16 * pair : 16 * pair + 16, j * LAGS : (j + 1) * LAGS] = both

    bytes_wait(fetched.at[0 : nc - 1], rsem.at[FETCH])
    sub = 8
    column_of = lax.rem(iota((LAGS, wide), 1), GROUP)

    @pl.loop(0, groups)
    def _(g):
        begin = pl.multiple_of(g * wide, wide)
        weights = jnp.dot(
            pick[pl.ds(begin, wide), :],
            fetched[...].reshape(slots + cells, hours),
            preferred_element_type=F32,
        ).astype(BF16)
        part[g] = jnp.zeros((nt, share, wide), F32)

        @pl.loop(0, GROUP // sub)
        def _(b):
            first = b * sub
            left = toep[pl.ds(g * GROUP + first, sub)].reshape(sub * LAGS, hours)
            sums = lax.dot_general(left, weights, (((1,), (1,)), ((), ())), preferred_element_type=F32)
            total = part[g].reshape(LAGS, wide)
            for s in range(sub):
                total = jnp.where(column_of == first + s, sums[s * LAGS : (s + 1) * LAGS], total)
            part[g] = total.reshape(nt, share, wide)

        @pl.loop(1, nt)
        def _(d):
            peer = lax.rem(tm + d, nt)
            remote(PART, part.at[g, nt - 1 - peer], got.at[tm, g], tm=peer).start()

    got[tm] = part[:, nt - 1 - tm]
    bytes_wait(got.at[0 : nt - 1], rsem.at[PART])

    whole = []
    for g in range(groups):
        total = got[0, g]
        for i in range(1, nt):
            total += got[i, g]
        whole.append(total)
    lag = tm * share + (share - 1) - iota((share, cells), 0)
    overlap = (valid_ref[...] - lag).astype(F32)
    lane_o = iota((share, cells), 1)
    each = cells // GROUP
    for k in range(refs):
        tile = k // each
        result = jnp.zeros((share, cells), F32)
        for g in range(groups):
            piece = whole[g][:, tile * cells : (tile + 1) * cells]
            shift = (GROUP * (g - k % each)) % cells
            if shift:
                piece = pltpu.roll(piece, shift, 1)
            result = jnp.where(lane_o // GROUP == g, piece, result)
        result = result / overlap
        for i in range(share):
            out_ref[share - 1 - i, k : k + 1, :] = result[i : i + 1]

    bytes_wait(req_in.at[0 : nc - 1], ssem.at[REQ])
    bytes_wait(stats.at[0 : nt - 1], ssem.at[STAT])

    @pl.when(tm > 0)
    def _():
        bytes_wait(halo_out, ssem.at[HALO])

    bytes_wait(fetched.at[0 : nc - 1], ssem.at[FETCH])
    bytes_wait(got.at[0 : nt - 1], ssem.at[PART])


def solution(mesh):
    nc, nt = mesh.shape["cells"], mesh.shape["tm"]

    def shards(urban, rural, urban_valid, rural_ids):
        hours, cells = urban.shape
        refs = rural_ids.shape[0]
        share = LAGS // nt
        groups, wide, slots = cells // GROUP, GROUP * refs, nc * CAP
        return pl.pallas_call(
            functools.partial(kernel, nc, nt),
            out_shape=jax.ShapeDtypeStruct((share, refs, cells), F32),
            in_specs=[pl.BlockSpec(memory_space=pltpu.VMEM)] * 4,
            out_specs=pl.BlockSpec(memory_space=pltpu.VMEM),
            scratch_shapes=[
                pltpu.VMEM((slots // cells, 1, cells), jnp.int32),
                pltpu.VMEM((nc, 1, cells), jnp.int32),
                pltpu.VMEM((GROUP, slots), F32),
                pltpu.VMEM((nt, 8, cells), F32),
                pltpu.VMEM((hours // LAGS + 1, cells, LAGS), F32),
                pltpu.VMEM((cells, LAGS), BF16),
                pltpu.VMEM((cells, LAGS), BF16),
                pltpu.VMEM((nc, CAP, hours), BF16),
                pltpu.VMEM((nc + cells // CAP, CAP, hours), BF16),
                pltpu.VMEM((cells * refs, slots + cells), BF16),
                pltpu.VMEM((cells, LAGS, hours), BF16),
                pltpu.VMEM((groups, nt, share, wide), F32),
                pltpu.VMEM((nt, groups, share, wide), F32),
                pltpu.SemaphoreType.DMA((5,)),
                pltpu.SemaphoreType.DMA((5,)),
            ],
            compiler_params=pltpu.CompilerParams(
                collective_id=0, has_side_effects=True, vmem_limit_bytes=48 * 1024 * 1024
            ),
        )(urban, rural, urban_valid.reshape(1, cells), rural_ids)

    in_specs = (P("tm", "cells"), P("tm", "cells"), P("cells"), P(None, "cells"))
    return jax.shard_map(
        shards, mesh=mesh, in_specs=in_specs, out_specs=P("tm", None, "cells"), check_vma=False
    )
```

time: 638 us -> 67.1 us (0.11)
  the two profiles are of different devices: /device:TPU:1 before, /device:TPU:30 now
where the time goes in v1:
time: 67.1 us; the launch traced here: 66.9 us
  Pallas kernels  63 us (94%)
  local copies, waits for them, and re-layouts  3.9 us (6%)
    pallas_call x1, Pallas kernels, shards(): pl.pallas_call(functools.partial(kernel, nc, nt), out_shape=jax.ShapeDtyp...  63 us
    unnamed x9, local copies, waits for them, and re-layouts  3.9 us

profile of v1, /device:TPU:30, one launch (start us, length us, event | category | flops | bytes accessed | tf_op | source)
XLA Modules:
  0.0 66.9 jit_solution(16254148668799834551)
XLA Ops:
  0.0 0.0 copy-start.3
  0.0 0.7 copy-done.3
  0.7 0.0 copy-start
  0.7 0.9 %copy-done = f32[512,128]{1,0:T(8,128)S(1)} copy-done((f32[512,128]{1,0:T(8,128)S(1)}, f32[512,128]{1,0:T(8,128)}, u32[]{:S(2)}) %copy-start) | copy-done | bytes 262168
  1.6 0.0 copy-start.1
  1.6 0.9 %copy-done.1 = f32[512,128]{1,0:T(8,128)S(1)} copy-done((f32[512,128]{1,0:T(8,128)S(1)}, f32[512,128]{1,0:T(8,128)}, u32[]{:S(2)}) %copy-start.1) | copy-done | bytes 262168
  2.6 0.0 copy-start.2
  2.6 0.7 %copy-done.2 = s32[8,128]{1,0:T(8,128)S(1)} copy-done((s32[8,128]{1,0:T(8,128)S(1)}, s32[8,128]{1,0:T(8,128)}, u32[]{:S(2)}) %copy-start.2) | copy-done | bytes 4120
  3.2 63.0 %shard_map.46 = f32[32,8,128]{2,1,0:T(8,128)S(1)} custom-call(f32[512,128]{1,0:T(8,128)S(1)} %copy-done, f32[512,128]{1,0:T(8,128)S(1)} %copy-done.1, s32[1,128]{1,0:T(1,128)S(1)} %bitcast.1, s32[8,128]{1,0:T(8,128)S(1)} %copy-done.2), custom_call_target="tpu_custom_call" | custom-call | tf_op jit(solution)/shard_map/pallas_call | solution.py:270
  66.3 0.7 copy.6
Async XLA Ops:
  0.0 0.7 copy-start.3
  0.7 0.9 %copy-start = (f32[512,128]{1,0:T(8,128)S(1)}, f32[512,128]{1,0:T(8,128)}, u32[]{:S(2)}) copy-start(f32[512,128]{1,0:T(8,128)} %urban_ref.1) | copy-start | bytes 786436
  1.6 0.9 %copy-start.1 = (f32[512,128]{1,0:T(8,128)S(1)}, f32[512,128]{1,0:T(8,128)}, u32[]{:S(2)}) copy-start(f32[512,128]{1,0:T(8,128)} %rural_ref.1) | copy-start | bytes 786436
  2.6 0.7 %copy-start.2 = (s32[8,128]{1,0:T(8,128)S(1)}, s32[8,128]{1,0:T(8,128)}, u32[]{:S(2)}) copy-start(s32[8,128]{1,0:T(8,128)} %ids_ref.1) | copy-start | bytes 12292

commit v2 on v1

v2 whole, which is shorter than its diff:
```python
import functools

import jax
import jax.numpy as jnp
from jax import lax
from jax.experimental import pallas as pl
from jax.experimental.pallas import tpu as pltpu
from jax.sharding import PartitionSpec as P

LAGS = 128
EPSILON = 1e-05
CAP = 16
GROUP = 32
PARTS = 2
MESH = pl.DeviceIdType.MESH
F32 = jnp.float32
BF16 = jnp.bfloat16

REQ, STAT, HALO, SUMS, TWIN, FETCH = 0, 1, 2, 3, 4, 4 + PARTS
KINDS = 4 + 2 * PARTS


def iota(shape, axis):
    return lax.broadcasted_iota(jnp.int32, shape, axis)


def bytes_wait(ref, sem):
    pltpu.make_async_copy(ref, ref, sem).wait()


def kernel(
    nc, nt, urban_hbm, rural_hbm, valid_ref, ids_ref, out_ref,
    urban_ref, rural_ref, req_out, req_in, req_acc, stats, ut, halo_out, halo_in,
    answer, choose, fetched, pick, toep, part, sums_out, sums_in, local_sem, ssem, rsem,
):
    hours, cells = urban_ref.shape
    refs = ids_ref.shape[0]
    share = LAGS // nt
    groups = cells // GROUP
    wide = GROUP * refs
    slots = nc * CAP
    half = nc // 2
    rows = cells // CAP
    span = hours // PARTS
    me = lax.axis_index("cells")
    tm = lax.axis_index("tm")
    side = me // half
    place = lax.rem(me, half)
    twin = (1 - side) * half + place

    def remote(kind, src, dst, **where):
        return pltpu.make_async_remote_copy(
            src_ref=src, dst_ref=dst, send_sem=ssem.at[kind], recv_sem=rsem.at[kind],
            device_id=where, device_id_type=MESH,
        )

    barrier = pltpu.get_barrier_semaphore()

    @pl.loop(1, nt)
    def _(d):
        pl.semaphore_signal(barrier, inc=1, device_id={"tm": lax.rem(tm + d, nt)}, device_id_type=MESH)

    pl.semaphore_signal(barrier, inc=1, device_id={"cells": twin}, device_id_type=MESH)

    @pl.loop(1, half)
    def _(d):
        peer = side * half + lax.rem(place + d, half)
        pl.semaphore_signal(barrier, inc=1, device_id={"cells": peer}, device_id_type=MESH)

    rural_in = pltpu.make_async_copy(rural_hbm, rural_ref, local_sem.at[0])
    urban_in = pltpu.make_async_copy(urban_hbm, urban_ref, local_sem.at[1])
    rural_in.start()
    urban_in.start()

    valid = valid_ref[...].astype(F32)
    hour = (tm * hours + iota((hours, cells), 0)).astype(F32)
    mask = (hour < valid).astype(F32)
    mine = stats.at[tm]
    rural_in.wait()
    rural = rural_ref[...]
    mine[2:3] = jnp.sum(rural, axis=0, keepdims=True)
    mine[3:4] = jnp.sum(rural * rural, axis=0, keepdims=True)
    urban_in.wait()
    urban = urban_ref[...]
    mine[0:1] = jnp.sum(urban * mask, axis=0, keepdims=True)
    mine[1:2] = jnp.sum(urban * urban * mask, axis=0, keepdims=True)
    mine[4:8] = jnp.zeros((4, cells), F32)

    pl.semaphore_wait(barrier, half - 1 + 1 + nt - 1)

    @pl.loop(1, nt)
    def _(d):
        remote(STAT, stats.at[tm], stats.at[tm], tm=lax.rem(tm + d, nt)).start()

    req_acc[...] = jnp.zeros_like(req_acc)
    owners = (ids_ref[...] >> 7).astype(F32)
    lane = iota((GROUP, cells), 1)
    row = iota((GROUP, cells), 0)
    mef = me.astype(F32)
    twinf = twin.astype(F32)
    sidef = side.astype(F32)

    @pl.loop(0, groups * refs, unroll=8)
    def _(block):
        g = block // refs
        k = block % refs
        one = lane == GROUP * g + row
        id_row = ids_ref[pl.ds(k, 1), :]
        owner = jnp.sum(jnp.where(one, (id_row >> 7).astype(F32), 0.0), axis=1, keepdims=True)
        local = jnp.sum(jnp.where(one, (id_row & 127).astype(F32), 0.0), axis=1, keepdims=True)
        order = k * cells + GROUP * g + row
        count = jnp.zeros((GROUP, cells), F32)
        for other in range(refs):
            earlier = (owners[other : other + 1] == owner) & (other * cells + lane < order)
            count += jnp.where(earlier, 1.0, 0.0)
        rank = jnp.sum(count, axis=1, keepdims=True)
        upper = jnp.where(owner >= half, 1.0, 0.0)
        away = jnp.where(upper == sidef, 0.0, 1.0)
        slot = ((owner - half * upper) * 2.0 + away) * CAP + rank
        slot = jnp.where(owner == mef, slots + local, jnp.where(owner == twinf, slots + cells + local, slot))
        slot = slot.astype(jnp.int32)
        begin = pl.multiple_of(block * GROUP, GROUP)
        for j in range(slots // cells + 2):
            hit = slot == lane + j * cells
            pick[pl.ds(begin, GROUP), j * cells : (j + 1) * cells] = jnp.where(hit, 1.0, 0.0).astype(BF16)
            if j < slots // cells:
                req_acc[:, j * cells : (j + 1) * cells] += jnp.where(hit, local, 0.0)

    asks = jnp.sum(req_acc[...], axis=0, keepdims=True).astype(jnp.int32)
    for j in range(slots // cells):
        req_out[j] = asks[:, j * cells : (j + 1) * cells]

    per = cells // (2 * CAP)

    @pl.loop(1, half)
    def _(d):
        other = lax.rem(place + d, half)
        remote(REQ, req_out.at[other // per], req_in.at[place], cells=side * half + other).start()

    req_in[place] = jnp.zeros((1, cells), jnp.int32)
    for p in range(PARTS):
        fetched[p, pl.ds(2 * place, 2)] = jnp.zeros((2, CAP, span), BF16)

    bytes_wait(stats.at[0 : nt - 1], rsem.at[STAT])
    total = stats[0]
    for i in range(1, nt):
        total += stats[i]

    def finish(series, first, second, n, keep):
        average = first / n
        spread = second / n - average * average
        return (series - average) * lax.rsqrt(spread + EPSILON) * keep

    rural_z = finish(rural_ref[...], total[2:3], total[3:4], F32(hours * nt), F32(1.0))
    for p in range(PARTS):
        turned = jnp.transpose(rural_z[p * span : (p + 1) * span]).astype(BF16)
        fetched[p, nc : nc + rows] = turned.reshape(rows, CAP, span)
        remote(
            TWIN + p, fetched.at[p, nc : nc + rows], fetched.at[p, nc + rows : nc + 2 * rows], cells=twin
        ).start()
    urban_z = finish(urban_ref[...], total[0:1], total[1:2], valid, mask)
    for j in range(hours // LAGS):
        ut[j] = jnp.transpose(urban_z[j * LAGS : (j + 1) * LAGS])
    halo_out[...] = ut[0].astype(BF16)

    @pl.when(tm > 0)
    def _():
        remote(HALO, halo_out, halo_in, tm=tm - 1).start()

    bytes_wait(req_in.at[0 : half - 1], rsem.at[REQ])
    batch = min(8, half)
    chunks = half // batch
    wanted = lax.rem(place, per) * 2 * CAP
    lane_c = iota((CAP, cells), 1)
    row_c = iota((CAP, cells), 0)
    here = [lane_c == wanted + rel * CAP + row_c for rel in range(2)]
    height = batch * CAP
    lane_h = iota((height, cells), 1)

    def respond(rel, p, q):
        block = fetched[p, nc + rel * rows : nc + (rel + 1) * rows].reshape(cells, span)
        begin = pl.multiple_of(q * height, height)
        chosen = jnp.dot(choose[rel, pl.ds(begin, height), :], block, preferred_element_type=F32)
        answer[p, rel, pl.ds(q * batch, batch)] = chosen.astype(BF16).reshape(batch, CAP, span)

        @pl.loop(0, batch)
        def _(s):
            other = q * batch + s

            @pl.when(other != place)
            def _():
                remote(
                    FETCH + p, answer.at[p, rel, other], fetched.at[p, 2 * place + rel], cells=side * half + other
                ).start()

    @pl.loop(0, chunks)
    def _(step):
        q = lax.rem(place // batch + step, chunks)
        begin = pl.multiple_of(q * height, height)
        for rel in range(2):
            columns = []
            for s in range(batch):
                asked = req_in[q * batch + s].astype(F32)
                columns.append(jnp.sum(jnp.where(here[rel], asked, 0.0), axis=1, keepdims=True))
            column = jnp.concatenate(columns, axis=0).astype(jnp.int32)
            choose[rel, pl.ds(begin, height), :] = jnp.where(column == lane_h, 1.0, 0.0).astype(BF16)
        for p in range(PARTS):
            respond(0, p, q)

    @pl.when(tm < nt - 1)
    def _():
        bytes_wait(halo_in, rsem.at[HALO])
        ut[hours // LAGS] = halo_in[...].astype(F32)

    @pl.when(tm == nt - 1)
    def _():
        ut[hours // LAGS] = jnp.zeros((cells, LAGS), F32)

    tiles = hours // LAGS
    lane8 = iota((8, LAGS), 1)
    row8 = iota((8, LAGS), 0)

    def build(first, last):
        @pl.loop(first, last, unroll=8)
        def _(c):
            wave = [jnp.broadcast_to(ut[j, pl.ds(c, 1), :], (8, LAGS)) for j in range(tiles + 1)]
            for pair in range(LAGS // 16):
                halves = []
                for a in (2 * pair, 2 * pair + 1):
                    turned = [pltpu.roll(x, 8 * a + 1, 1, stride=1, stride_axis=0) for x in wave]
                    upper = lane8 >= row8 + (8 * a + 1)
                    halves.append([jnp.where(upper, turned[j + 1], turned[j]) for j in range(tiles)])
                for j in range(tiles):
                    both = jnp.concatenate([halves[0][j], halves[1][j]], axis=0).astype(BF16)
                    at = (j * LAGS) % span
                    toep[(j * LAGS) // span, c, 16 * pair : 16 * pair + 16, at : at + LAGS] = both

    build(0, cells // 2)
    for p in range(PARTS):
        bytes_wait(fetched.at[p, nc + rows : nc + 2 * rows], rsem.at[TWIN + p])

        @pl.loop(0, chunks)
        def _(step):
            respond(1, p, lax.rem(place // batch + step, chunks))

    build(cells // 2, cells)

    column_of = lax.rem(iota((LAGS, wide), 1), GROUP)
    for p in range(PARTS):
        bytes_wait(fetched.at[p, 0 : nc - 2], rsem.at[FETCH + p])

        @pl.loop(0, groups)
        def _(g):
            begin = pl.multiple_of(g * wide, wide)
            weights = jnp.dot(
                pick[pl.ds(begin, wide), :],
                fetched[p].reshape(slots + 2 * cells, span),
                preferred_element_type=F32,
            ).astype(BF16)
            left = toep[p, pl.ds(g * GROUP, GROUP)].reshape(GROUP * LAGS, span)
            sums = lax.dot_general(left, weights, (((1,), (1,)), ((), ())), preferred_element_type=F32)
            total = sums[0:LAGS]
            for s in range(1, GROUP):
                total = jnp.where(column_of == s, sums[s * LAGS : (s + 1) * LAGS], total)
            if p:
                total += part[g].reshape(LAGS, wide)
            part[g] = total.reshape(nt, share, wide)
            if p == PARTS - 1:
                sums_out[g] = total.astype(BF16).reshape(nt, share, wide)

                @pl.loop(1, nt)
                def _(d):
                    peer = lax.rem(tm + d, nt)
                    remote(SUMS, sums_out.at[g, nt - 1 - peer], sums_in.at[tm, g], tm=peer).start()

    sums_in[tm] = jnp.zeros((groups, share, wide), BF16)
    bytes_wait(sums_in.at[0 : nt - 1], rsem.at[SUMS])

    whole = []
    for g in range(groups):
        total = part[g, nt - 1 - tm]
        for i in range(nt):
            total += sums_in[i, g].astype(F32)
        whole.append(total)
    lag = tm * share + (share - 1) - iota((share, cells), 0)
    overlap = (valid_ref[...] - lag).astype(F32)
    lane_o = iota((share, cells), 1)
    each = cells // GROUP
    for k in range(refs):
        tile = k // each
        result = jnp.zeros((share, cells), F32)
        for g in range(groups):
            piece = whole[g][:, tile * cells : (tile + 1) * cells]
            shift = (GROUP * (g - k % each)) % cells
            if shift:
                piece = pltpu.roll(piece, shift, 1)
            result = jnp.where(lane_o // GROUP == g, piece, result)
        result = result / overlap
        for i in range(share):
            out_ref[share - 1 - i, k : k + 1, :] = result[i : i + 1]

    bytes_wait(req_in.at[0 : half - 1], ssem.at[REQ])
    bytes_wait(stats.at[0 : nt - 1], ssem.at[STAT])

    @pl.when(tm > 0)
    def _():
        bytes_wait(halo_out, ssem.at[HALO])

    for p in range(PARTS):
        bytes_wait(fetched.at[p, nc : nc + rows], ssem.at[TWIN + p])
        bytes_wait(fetched.at[p, 0 : nc - 2], ssem.at[FETCH + p])
    bytes_wait(sums_in.at[0 : nt - 1], ssem.at[SUMS])


def solution(mesh):
    nc, nt = mesh.shape["cells"], mesh.shape["tm"]

    def shards(urban, rural, urban_valid, rural_ids):
        hours, cells = urban.shape
        refs = rural_ids.shape[0]
        share = LAGS // nt
        groups, wide, slots, half = cells // GROUP, GROUP * refs, nc * CAP, nc // 2
        span, rows = hours // PARTS, cells // CAP
        vmem = pl.BlockSpec(memory_space=pltpu.VMEM)
        whole = pl.BlockSpec(memory_space=pl.ANY)
        return pl.pallas_call(
            functools.partial(kernel, nc, nt),
            out_shape=jax.ShapeDtypeStruct((share, refs, cells), F32),
            in_specs=[whole, whole, vmem, vmem],
            out_specs=vmem,
            scratch_shapes=[
                pltpu.VMEM((hours, cells), F32),
                pltpu.VMEM((hours, cells), F32),
                pltpu.VMEM((slots // cells, 1, cells), jnp.int32),
                pltpu.VMEM((half, 1, cells), jnp.int32),
                pltpu.VMEM((GROUP, slots), F32),
                pltpu.VMEM((nt, 8, cells), F32),
                pltpu.VMEM((hours // LAGS + 1, cells, LAGS), F32),
                pltpu.VMEM((cells, LAGS), BF16),
                pltpu.VMEM((cells, LAGS), BF16),
                pltpu.VMEM((PARTS, 2, half, CAP, span), BF16),
                pltpu.VMEM((2, half * CAP, cells), BF16),
                pltpu.VMEM((PARTS, nc + 2 * rows, CAP, span), BF16),
                pltpu.VMEM((cells * refs, slots + 2 * cells), BF16),
                pltpu.VMEM((PARTS, cells, LAGS, span), BF16),
                pltpu.VMEM((groups, nt, share, wide), F32),
                pltpu.VMEM((groups, nt, share, wide), BF16),
                pltpu.VMEM((nt, groups, share, wide), BF16),
                pltpu.SemaphoreType.DMA((2,)),
                pltpu.SemaphoreType.DMA((KINDS,)),
                pltpu.SemaphoreType.DMA((KINDS,)),
            ],
            compiler_params=pltpu.CompilerParams(
                collective_id=0, has_side_effects=True, vmem_limit_bytes=52 * 1024 * 1024
            ),
        )(urban, rural, urban_valid.reshape(1, cells), rural_ids)

    in_specs = (P("tm", "cells"), P("tm", "cells"), P("cells"), P(None, "cells"))
    return jax.shard_map(
        shards, mesh=mesh, in_specs=in_specs, out_specs=P("tm", None, "cells"), check_vma=False
    )
```

time: 67.1 us -> 50.3 us (0.75)
  the two profiles are of different devices: /device:TPU:30 before, /device:TPU:1 now
where the time goes in v2:
time: 50.3 us; the launch traced here: 50.2 us
  Pallas kernels  46.2 us (92%)
  local copies, waits for them, and re-layouts  3.9 us (8%)
    pallas_call x1, Pallas kernels, shards(): pl.pallas_call(functools.partial(kernel, nc, nt), out_shape=jax.ShapeDtyp...  46.2 us
    unnamed x9, local copies, waits for them, and re-layouts  3.9 us

profile of v2, /device:TPU:1, one launch (start us, length us, event | category | flops | bytes accessed | tf_op | source)
XLA Modules:
  0.0 50.2 jit_solution(9411762696348865145)
XLA Ops:
  0.0 0.0 copy-start.3
  0.0 0.7 %copy-done.3 = s32[128]{0:T(128)S(1)} copy-done((s32[128]{0:T(128)S(1)}, s32[128]{0:T(128)}, u32[]{:S(2)}) %copy-start.3) | copy-done | bytes 536
  0.7 0.0 copy-start
  0.7 0.9 %copy-done = f32[512,128]{1,0:T(8,128)S(1)} copy-done((f32[512,128]{1,0:T(8,128)S(1)}, f32[512,128]{1,0:T(8,128)}, u32[]{:S(2)}) %copy-start) | copy-done | bytes 262168
  1.6 0.0 copy-start.1
  1.6 0.9 %copy-done.1 = f32[512,128]{1,0:T(8,128)S(1)} copy-done((f32[512,128]{1,0:T(8,128)S(1)}, f32[512,128]{1,0:T(8,128)}, u32[]{:S(2)}) %copy-start.1) | copy-done | bytes 262168
  2.6 0.0 copy-start.2
  2.6 0.7 %copy-done.2 = s32[8,128]{1,0:T(8,128)S(1)} copy-done((s32[8,128]{1,0:T(8,128)S(1)}, s32[8,128]{1,0:T(8,128)}, u32[]{:S(2)}) %copy-start.2) | copy-done | bytes 4120
  3.2 46.2 %shard_map.46 = f32[32,8,128]{2,1,0:T(8,128)S(1)} custom-call(f32[512,128]{1,0:T(8,128)S(1)} %copy-done, f32[512,128]{1,0:T(8,128)S(1)} %copy-done.1, s32[1,128]{1,0:T(1,128)S(1)} %bitcast.1, s32[8,128]{1,0:T(8,128)S(1)} %copy-done.2), custom_call_target="tpu_custom_call" | custom-call | tf_op jit(solution)/shard_map/pallas_call | solution.py:326
  49.5 0.7 %copy.6 = f32[32,8,128]{2,1,0:T(8,128)} copy(f32[32,8,128]{2,1,0:T(8,128)S(1)} %shard_map.46) | data formatting | bytes 262144
Async XLA Ops:
  0.0 0.7 %copy-start.3 = (s32[128]{0:T(128)S(1)}, s32[128]{0:T(128)}, u32[]{:S(2)}) copy-start(s32[128]{0:T(128)} %param.6) | copy-start | bytes 1540
  0.7 0.9 %copy-start = (f32[512,128]{1,0:T(8,128)S(1)}, f32[512,128]{1,0:T(8,128)}, u32[]{:S(2)}) copy-start(f32[512,128]{1,0:T(8,128)} %urban_hbm.1) | copy-start | bytes 786436
  1.6 0.9 %copy-start.1 = (f32[512,128]{1,0:T(8,128)S(1)}, f32[512,128]{1,0:T(8,128)}, u32[]{:S(2)}) copy-start(f32[512,128]{1,0:T(8,128)} %rural_hbm.1) | copy-start | bytes 786436
  2.6 0.7 %copy-start.2 = (s32[8,128]{1,0:T(8,128)S(1)}, s32[8,128]{1,0:T(8,128)}, u32[]{:S(2)}) copy-start(s32[8,128]{1,0:T(8,128)} %ids_ref.1) | copy-start | bytes 12292

commit v3 on v2

--- a/solution.py
+++ b/solution.py
@@ -16,8 +16,9 @@
 F32 = jnp.float32
 BF16 = jnp.bfloat16
 
-REQ, STAT, HALO, SUMS, TWIN, FETCH = 0, 1, 2, 3, 4, 4 + PARTS
-KINDS = 4 + 2 * PARTS
+REQ, STAT, HALO, SUMS, PEAK, TWIN, FETCH = 0, 1, 2, 3, 4, 5, 5 + PARTS
+KINDS = 5 + 2 * PARTS
+TOP = 32760.0
 
 
 def iota(shape, axis):
@@ -30,8 +31,8 @@
 
 def kernel(
     nc, nt, urban_hbm, rural_hbm, valid_ref, ids_ref, out_ref,
-    urban_ref, rural_ref, req_out, req_in, req_acc, stats, ut, halo_out, halo_in,
-    answer, choose, fetched, pick, toep, part, sums_out, sums_in, local_sem, ssem, rsem,
+    urban_ref, rural_ref, req_out, req_in, slot_rows, stats, ut, halo_out, halo_in,
+    answer, choose, fetched, pick, toep, part, sums_out, sums_in, peak_out, peak_in, local_sem, ssem, rsem,
 ):
     hours, cells = urban_ref.shape
     refs = ids_ref.shape[0]
@@ -72,6 +73,38 @@
     rural_in.start()
     urban_in.start()
 
+    ids = ids_ref[...]
+    owner = (ids >> 7).astype(F32)
+    local = (ids & 127).astype(F32)
+    upper = jnp.where(owner >= half, 1.0, 0.0)
+    away = jnp.where(upper == side.astype(F32), 0.0, 1.0)
+    home = (owner - half * upper) * 2.0 + away
+    home_i = iota((nc, cells), 0).astype(F32)
+    belongs = [jnp.where(home[k : k + 1] == home_i, 1.0, 0.0) for k in range(refs)]
+    earlier = iota((cells, 2 * cells), 0) < iota((cells, 2 * cells), 1)
+    counts = jnp.dot(
+        jnp.concatenate(belongs, axis=0).astype(BF16), jnp.where(earlier, 1.0, 0.0).astype(BF16),
+        preferred_element_type=F32,
+    )
+    before = jnp.zeros((nc, cells), F32)
+    rank_i = iota((cells, cells), 0).astype(F32)
+    asks = jnp.zeros((nc, cells), F32)
+    for k in range(refs):
+        count = counts[k * nc : (k + 1) * nc]
+        rank = jnp.sum(belongs[k] * (count[:, 0:cells] + before), axis=0, keepdims=True)
+        before += count[:, cells : 2 * cells]
+        wish = jnp.where(rank == rank_i, local[k : k + 1], 0.0).astype(BF16)
+        asks += lax.dot_general(
+            belongs[k].astype(BF16), wish, (((1,), (1,)), ((), ())), preferred_element_type=F32
+        )
+        slot = home[k : k + 1] * CAP + rank
+        slot = jnp.where(owner[k : k + 1] == me.astype(F32), slots + local[k : k + 1], slot)
+        slot = jnp.where(owner[k : k + 1] == twin.astype(F32), slots + cells + local[k : k + 1], slot)
+        slot_rows[k : k + 1] = slot
+    asks = asks.astype(jnp.int32)
+    for q in range(half):
+        req_out[q] = asks[2 * q : 2 * q + 2]
+
     valid = valid_ref[...].astype(F32)
     hour = (tm * hours + iota((hours, cells), 0)).astype(F32)
     mask = (hour < valid).astype(F32)
@@ -92,52 +125,27 @@
     def _(d):
         remote(STAT, stats.at[tm], stats.at[tm], tm=lax.rem(tm + d, nt)).start()
 
-    req_acc[...] = jnp.zeros_like(req_acc)
-    owners = (ids_ref[...] >> 7).astype(F32)
+
+    @pl.loop(1, half)
+    def _(d):
+        other = lax.rem(place + d, half)
+        remote(REQ, req_out.at[other], req_in.at[place], cells=side * half + other).start()
+
+    req_in[place] = jnp.zeros((2, cells), jnp.int32)
+
     lane = iota((GROUP, cells), 1)
     row = iota((GROUP, cells), 0)
-    mef = me.astype(F32)
-    twinf = twin.astype(F32)
-    sidef = side.astype(F32)
 
     @pl.loop(0, groups * refs, unroll=8)
     def _(block):
-        g = block // refs
-        k = block % refs
-        one = lane == GROUP * g + row
-        id_row = ids_ref[pl.ds(k, 1), :]
-        owner = jnp.sum(jnp.where(one, (id_row >> 7).astype(F32), 0.0), axis=1, keepdims=True)
-        local = jnp.sum(jnp.where(one, (id_row & 127).astype(F32), 0.0), axis=1, keepdims=True)
-        order = k * cells + GROUP * g + row
-        count = jnp.zeros((GROUP, cells), F32)
-        for other in range(refs):
-            earlier = (owners[other : other + 1] == owner) & (other * cells + lane < order)
-            count += jnp.where(earlier, 1.0, 0.0)
-        rank = jnp.sum(count, axis=1, keepdims=True)
-        upper = jnp.where(owner >= half, 1.0, 0.0)
-        away = jnp.where(upper == sidef, 0.0, 1.0)
-        slot = ((owner - half * upper) * 2.0 + away) * CAP + rank
-        slot = jnp.where(owner == mef, slots + local, jnp.where(owner == twinf, slots + cells + local, slot))
-        slot = slot.astype(jnp.int32)
+        one = lane == GROUP * (block // refs) + row
+        slot_row = slot_rows[pl.ds(block % refs, 1), :]
+        slot = jnp.sum(jnp.where(one, slot_row, 0.0), axis=1, keepdims=True).astype(jnp.int32)
         begin = pl.multiple_of(block * GROUP, GROUP)
         for j in range(slots // cells + 2):
             hit = slot == lane + j * cells
             pick[pl.ds(begin, GROUP), j * cells : (j + 1) * cells] = jnp.where(hit, 1.0, 0.0).astype(BF16)
-            if j < slots // cells:
-                req_acc[:, j * cells : (j + 1) * cells] += jnp.where(hit, local, 0.0)
-
-    asks = jnp.sum(req_acc[...], axis=0, keepdims=True).astype(jnp.int32)
-    for j in range(slots // cells):
-        req_out[j] = asks[:, j * cells : (j + 1) * cells]
-
-    per = cells // (2 * CAP)
-
-    @pl.loop(1, half)
-    def _(d):
-        other = lax.rem(place + d, half)
-        remote(REQ, req_out.at[other // per], req_in.at[place], cells=side * half + other).start()
-
-    req_in[place] = jnp.zeros((1, cells), jnp.int32)
+
     for p in range(PARTS):
         fetched[p, pl.ds(2 * place, 2)] = jnp.zeros((2, CAP, span), BF16)
 
@@ -170,10 +178,9 @@
     bytes_wait(req_in.at[0 : half - 1], rsem.at[REQ])
     batch = min(8, half)
     chunks = half // batch
-    wanted = lax.rem(place, per) * 2 * CAP
     lane_c = iota((CAP, cells), 1)
     row_c = iota((CAP, cells), 0)
-    here = [lane_c == wanted + rel * CAP + row_c for rel in range(2)]
+    here = lane_c == row_c
     height = batch * CAP
     lane_h = iota((height, cells), 1)
 
@@ -192,6 +199,11 @@
                 remote(
                     FETCH + p, answer.at[p, rel, other], fetched.at[p, 2 * place + rel], cells=side * half + other
                 ).start()
+
+    def respond_all(rel, p):
+        @pl.loop(0, chunks)
+        def _(step):
+            respond(rel, p, lax.rem(place // batch + step, chunks))
 
     @pl.loop(0, chunks)
     def _(step):
@@ -200,12 +212,14 @@
         for rel in range(2):
             columns = []
             for s in range(batch):
-                asked = req_in[q * batch + s].astype(F32)
-                columns.append(jnp.sum(jnp.where(here[rel], asked, 0.0), axis=1, keepdims=True))
+                asked = req_in[q * batch + s][rel : rel + 1].astype(F32)
+                columns.append(jnp.sum(jnp.where(here, asked, 0.0), axis=1, keepdims=True))
             column = jnp.concatenate(columns, axis=0).astype(jnp.int32)
             choose[rel, pl.ds(begin, height), :] = jnp.where(column == lane_h, 1.0, 0.0).astype(BF16)
-        for p in range(PARTS):
-            respond(0, p, q)
+        respond(0, 0, q)
+
+    for p in range(1, PARTS):
+        respond_all(0, p)
 
     @pl.when(tm < nt - 1)
     def _():
@@ -235,13 +249,11 @@
                     at = (j * LAGS) % span
                     toep[(j * LAGS) // span, c, 16 * pair : 16 * pair + 16, at : at + LAGS] = both
 
-    build(0, cells // 2)
-    for p in range(PARTS):
+    step = cells // (2 * PARTS)
+    for p in range(PARTS):
+        build(p * step, (p + 1) * step)
         bytes_wait(fetched.at[p, nc + rows : nc + 2 * rows], rsem.at[TWIN + p])
-
-        @pl.loop(0, chunks)
-        def _(step):
-            respond(1, p, lax.rem(place // batch + step, chunks))
+        respond_all(1, p)
 
     build(cells // 2, cells)
 
@@ -266,21 +278,27 @@
                 total += part[g].reshape(LAGS, wide)
             part[g] = total.reshape(nt, share, wide)
             if p == PARTS - 1:
-                sums_out[g] = total.astype(BF16).reshape(nt, share, wide)
+                peak = jnp.maximum(jnp.max(jnp.abs(total), axis=0, keepdims=True), 1e-30)
+                peak_out[g] = peak
+                coded = jnp.floor(total * (TOP / peak) + 0.5).astype(jnp.int32).astype(jnp.int16)
+                sums_out[g] = coded.reshape(nt, share, wide)
 
                 @pl.loop(1, nt)
                 def _(d):
                     peer = lax.rem(tm + d, nt)
                     remote(SUMS, sums_out.at[g, nt - 1 - peer], sums_in.at[tm, g], tm=peer).start()
-
-    sums_in[tm] = jnp.zeros((groups, share, wide), BF16)
+                    remote(PEAK, peak_out.at[g], peak_in.at[tm, g], tm=peer).start()
+
+    sums_in[tm] = jnp.zeros((groups, share, wide), jnp.int16)
+    peak_in[tm] = jnp.zeros((groups, 1, wide), F32)
     bytes_wait(sums_in.at[0 : nt - 1], rsem.at[SUMS])
+    bytes_wait(peak_in.at[0 : nt - 1], rsem.at[PEAK])
 
     whole = []
     for g in range(groups):
         total = part[g, nt - 1 - tm]
         for i in range(nt):
-            total += sums_in[i, g].astype(F32)
+            total += sums_in[i, g].astype(jnp.int32).astype(F32) * (peak_in[i, g] * (1.0 / TOP))
         whole.append(total)
     lag = tm * share + (share - 1) - iota((share, cells), 0)
     overlap = (valid_ref[...] - lag).astype(F32)
@@ -310,6 +328,7 @@
         bytes_wait(fetched.at[p, nc : nc + rows], ssem.at[TWIN + p])
         bytes_wait(fetched.at[p, 0 : nc - 2], ssem.at[FETCH + p])
     bytes_wait(sums_in.at[0 : nt - 1], ssem.at[SUMS])
+    bytes_wait(peak_in.at[0 : nt - 1], ssem.at[PEAK])
 
 
 def solution(mesh):
@@ -331,9 +350,9 @@
             scratch_shapes=[
                 pltpu.VMEM((hours, cells), F32),
                 pltpu.VMEM((hours, cells), F32),
-                pltpu.VMEM((slots // cells, 1, cells), jnp.int32),
-                pltpu.VMEM((half, 1, cells), jnp.int32),
-                pltpu.VMEM((GROUP, slots), F32),
+                pltpu.VMEM((half, 2, cells), jnp.int32),
+                pltpu.VMEM((half, 2, cells), jnp.int32),
+                pltpu.VMEM((refs, cells), F32),
                 pltpu.VMEM((nt, 8, cells), F32),
                 pltpu.VMEM((hours // LAGS + 1, cells, LAGS), F32),
                 pltpu.VMEM((cells, LAGS), BF16),
@@ -344,8 +363,10 @@
                 pltpu.VMEM((cells * refs, slots + 2 * cells), BF16),
                 pltpu.VMEM((PARTS, cells, LAGS, span), BF16),
                 pltpu.VMEM((groups, nt, share, wide), F32),
-                pltpu.VMEM((groups, nt, share, wide), BF16),
-                pltpu.VMEM((nt, groups, share, wide), BF16),
+                pltpu.VMEM((groups, nt, share, wide), jnp.int16),
+                pltpu.VMEM((nt, groups, share, wide), jnp.int16),
+                pltpu.VMEM((groups, 1, wide), F32),
+                pltpu.VMEM((nt, groups, 1, wide), F32),
                 pltpu.SemaphoreType.DMA((2,)),
                 pltpu.SemaphoreType.DMA((KINDS,)),
                 pltpu.SemaphoreType.DMA((KINDS,)),

time: 50.3 us -> 48 us (0.954)
  Pallas kernels: 46.2 us -> 43.9 us
    pallas_call x1, Pallas kernels: 46.2 us -> 43.9 us  [shards(): pl.pallas_call(functools.partial(kernel, nc, nt), out_shape=jax.ShapeDtyp...]
where the time goes in v3:
time: 48 us; the launch traced here: 47.8 us
  Pallas kernels  43.9 us (91%)
  local copies, waits for them, and re-layouts  3.9 us (8%)
    pallas_call x1, Pallas kernels, shards(): pl.pallas_call(functools.partial(kernel, nc, nt), out_shape=jax.ShapeDtyp...  43.9 us
    unnamed x9, local copies, waits for them, and re-layouts  3.9 us

profile of v3, /device:TPU:1, one launch (start us, length us, event | category | flops | bytes accessed | tf_op | source)
XLA Modules:
  0.0 47.8 jit_solution(7921244726124386204)
XLA Ops:
  0.0 0.0 copy-start.3
  0.0 0.7 %copy-done.3 = s32[128]{0:T(128)S(1)} copy-done((s32[128]{0:T(128)S(1)}, s32[128]{0:T(128)}, u32[]{:S(2)}) %copy-start.3) | copy-done | bytes 536
  0.7 0.0 copy-start
  0.7 0.9 %copy-done = f32[512,128]{1,0:T(8,128)S(1)} copy-done((f32[512,128]{1,0:T(8,128)S(1)}, f32[512,128]{1,0:T(8,128)}, u32[]{:S(2)}) %copy-start) | copy-done | bytes 262168
  1.6 0.0 copy-start.1
  1.6 0.9 %copy-done.1 = f32[512,128]{1,0:T(8,128)S(1)} copy-done((f32[512,128]{1,0:T(8,128)S(1)}, f32[512,128]{1,0:T(8,128)}, u32[]{:S(2)}) %copy-start.1) | copy-done | bytes 262168
  2.6 0.0 copy-start.2
  2.6 0.7 %copy-done.2 = s32[8,128]{1,0:T(8,128)S(1)} copy-done((s32[8,128]{1,0:T(8,128)S(1)}, s32[8,128]{1,0:T(8,128)}, u32[]{:S(2)}) %copy-start.2) | copy-done | bytes 4120
  3.2 43.9 %shard_map.46 = f32[32,8,128]{2,1,0:T(8,128)S(1)} custom-call(f32[512,128]{1,0:T(8,128)S(1)} %copy-done, f32[512,128]{1,0:T(8,128)S(1)} %copy-done.1, s32[1,128]{1,0:T(1,128)S(1)} %bitcast.1, s32[8,128]{1,0:T(8,128)S(1)} %copy-done.2), custom_call_target="tpu_custom_call" | custom-call | tf_op jit(solution)/shard_map/pallas_call | solution.py:345
  47.2 0.7 %copy.6 = f32[32,8,128]{2,1,0:T(8,128)} copy(f32[32,8,128]{2,1,0:T(8,128)S(1)} %shard_map.46) | data formatting | bytes 262144
Async XLA Ops:
  0.0 0.7 %copy-start.3 = (s32[128]{0:T(128)S(1)}, s32[128]{0:T(128)}, u32[]{:S(2)}) copy-start(s32[128]{0:T(128)} %param.6) | copy-start | bytes 1540
  0.7 0.9 %copy-start = (f32[512,128]{1,0:T(8,128)S(1)}, f32[512,128]{1,0:T(8,128)}, u32[]{:S(2)}) copy-start(f32[512,128]{1,0:T(8,128)} %urban_hbm.1) | copy-start | bytes 786436
  1.6 0.9 %copy-start.1 = (f32[512,128]{1,0:T(8,128)S(1)}, f32[512,128]{1,0:T(8,128)}, u32[]{:S(2)}) copy-start(f32[512,128]{1,0:T(8,128)} %rural_hbm.1) | copy-start | bytes 786436
  2.6 0.7 %copy-start.2 = (s32[8,128]{1,0:T(8,128)S(1)}, s32[8,128]{1,0:T(8,128)}, u32[]{:S(2)}) copy-start(s32[8,128]{1,0:T(8,128)} %ids_ref.1) | copy-start | bytes 12292

commit v4 on v3

--- a/solution.py
+++ b/solution.py
@@ -10,7 +10,7 @@
 LAGS = 128
 EPSILON = 1e-05
 CAP = 16
-GROUP = 32
+GROUP = 8
 PARTS = 2
 MESH = pl.DeviceIdType.MESH
 F32 = jnp.float32
@@ -32,13 +32,14 @@
 def kernel(
     nc, nt, urban_hbm, rural_hbm, valid_ref, ids_ref, out_ref,
     urban_ref, rural_ref, req_out, req_in, slot_rows, stats, ut, halo_out, halo_in,
-    answer, choose, fetched, pick, toep, part, sums_out, sums_in, peak_out, peak_in, local_sem, ssem, rsem,
+    answer, choose, fetched, pick, toep, moved, part, kept, sums_out, sums_in, peak_out, peak_in, local_sem, ssem, rsem,
 ):
     hours, cells = urban_ref.shape
     refs = ids_ref.shape[0]
     share = LAGS // nt
     groups = cells // GROUP
     wide = GROUP * refs
+    quads = groups // 4
     slots = nc * CAP
     half = nc // 2
     rows = cells // CAP
@@ -135,16 +136,18 @@
 
     lane = iota((GROUP, cells), 1)
     row = iota((GROUP, cells), 0)
-
-    @pl.loop(0, groups * refs, unroll=8)
-    def _(block):
-        one = lane == GROUP * (block // refs) + row
-        slot_row = slot_rows[pl.ds(block % refs, 1), :]
-        slot = jnp.sum(jnp.where(one, slot_row, 0.0), axis=1, keepdims=True).astype(jnp.int32)
-        begin = pl.multiple_of(block * GROUP, GROUP)
+    lane_w = iota((wide, cells), 1)
+
+    @pl.loop(0, groups, unroll=4)
+    def _(g):
+        one = lane == GROUP * g + row
+        table = slot_rows[...]
+        each = [jnp.where(one, table[k : k + 1], 0.0) for k in range(refs)]
+        slot = jnp.sum(jnp.concatenate(each, axis=0), axis=1, keepdims=True).astype(jnp.int32)
+        begin = pl.multiple_of(g * wide, wide)
         for j in range(slots // cells + 2):
-            hit = slot == lane + j * cells
-            pick[pl.ds(begin, GROUP), j * cells : (j + 1) * cells] = jnp.where(hit, 1.0, 0.0).astype(BF16)
+            hit = slot == lane_w + j * cells
+            pick[pl.ds(begin, wide), j * cells : (j + 1) * cells] = jnp.where(hit, 1.0, 0.0).astype(BF16)
 
     for p in range(PARTS):
         fetched[p, pl.ds(2 * place, 2)] = jnp.zeros((2, CAP, span), BF16)
@@ -238,16 +241,17 @@
         @pl.loop(first, last, unroll=8)
         def _(c):
             wave = [jnp.broadcast_to(ut[j, pl.ds(c, 1), :], (8, LAGS)) for j in range(tiles + 1)]
-            for pair in range(LAGS // 16):
+            for pair in range(share // 16):
                 halves = []
                 for a in (2 * pair, 2 * pair + 1):
-                    turned = [pltpu.roll(x, 8 * a + 1, 1, stride=1, stride_axis=0) for x in wave]
-                    upper = lane8 >= row8 + (8 * a + 1)
-                    halves.append([jnp.where(upper, turned[j + 1], turned[j]) for j in range(tiles)])
-                for j in range(tiles):
+                    shift = LAGS - share + 1 + 8 * a
+                    turned = [pltpu.roll(x, shift, 1, stride=1, stride_axis=0) for x in wave]
+                    turned.append(jnp.zeros((8, LAGS), F32))
+                    upper = lane8 >= row8 + shift
+                    halves.append([jnp.where(upper, turned[j + 1], turned[j]) for j in range(tiles + 1)])
+                for j in range(tiles + 1):
                     both = jnp.concatenate([halves[0][j], halves[1][j]], axis=0).astype(BF16)
-                    at = (j * LAGS) % span
-                    toep[(j * LAGS) // span, c, 16 * pair : 16 * pair + 16, at : at + LAGS] = both
+                    toep[c, 16 * pair : 16 * pair + 16, j * LAGS : (j + 1) * LAGS] = both
 
     step = cells // (2 * PARTS)
     for p in range(PARTS):
@@ -257,62 +261,98 @@
 
     build(cells // 2, cells)
 
-    column_of = lax.rem(iota((LAGS, wide), 1), GROUP)
+    column_of = lax.rem(iota((share, nt * wide), 1), GROUP)
+    lane_t = iota((4 * wide, LAGS), 1)
+    lane_s = iota((share, 2 * wide), 1)
+    reach = span + LAGS
     for p in range(PARTS):
         bytes_wait(fetched.at[p, 0 : nc - 2], rsem.at[FETCH + p])
 
-        @pl.loop(0, groups)
-        def _(g):
-            begin = pl.multiple_of(g * wide, wide)
-            weights = jnp.dot(
-                pick[pl.ds(begin, wide), :],
+        @pl.loop(0, quads)
+        def _(quad):
+            begin = pl.multiple_of(quad * 4 * wide, 4 * wide)
+            chosen = jnp.dot(
+                pick[pl.ds(begin, 4 * wide), :],
                 fetched[p].reshape(slots + 2 * cells, span),
                 preferred_element_type=F32,
-            ).astype(BF16)
-            left = toep[p, pl.ds(g * GROUP, GROUP)].reshape(GROUP * LAGS, span)
-            sums = lax.dot_general(left, weights, (((1,), (1,)), ((), ())), preferred_element_type=F32)
-            total = sums[0:LAGS]
-            for s in range(1, GROUP):
-                total = jnp.where(column_of == s, sums[s * LAGS : (s + 1) * LAGS], total)
-            if p:
-                total += part[g].reshape(LAGS, wide)
-            part[g] = total.reshape(nt, share, wide)
+            )
+            pieces = [chosen[:, j * LAGS : (j + 1) * LAGS] for j in range(span // LAGS)]
+            none = jnp.zeros((4 * wide, LAGS), F32)
+            for a in range(nt):
+                shift = share * a
+                turned = [none] + [pltpu.roll(x, shift, 1) if a else x for x in pieces] + [none]
+                for j in range(span // LAGS + 1):
+                    piece = jnp.where(lane_t >= shift, turned[j + 1], turned[j]) if a else turned[j + 1]
+                    piece = piece.astype(BF16)
+                    for i in range(4):
+                        moved[i, a, :, j * LAGS : (j + 1) * LAGS] = piece[i * wide : (i + 1) * wide]
+            totals = []
+            for i in range(4):
+                g = 4 * quad + i
+                left = toep[pl.ds(GROUP * g, GROUP), :, p * span : p * span + reach].reshape(GROUP * share, reach)
+                sums = lax.dot_general(
+                    left, moved[i].reshape(nt * wide, reach), (((1,), (1,)), ((), ())), preferred_element_type=F32
+                )
+                total = sums[0:share]
+                for c in range(1, GROUP):
+                    total = jnp.where(column_of == c, sums[c * share : (c + 1) * share], total)
+                if p:
+                    total += part[g]
+                if p < PARTS - 1:
+                    part[g] = total
+                totals.append(total)
             if p == PARTS - 1:
-                peak = jnp.maximum(jnp.max(jnp.abs(total), axis=0, keepdims=True), 1e-30)
-                peak_out[g] = peak
-                coded = jnp.floor(total * (TOP / peak) + 0.5).astype(jnp.int32).astype(jnp.int16)
-                sums_out[g] = coded.reshape(nt, share, wide)
+                for h in range(2):
+                    even, odd = totals[2 * h], totals[2 * h + 1]
+                    blocks = []
+                    for a in range(nt):
+                        at = (a // 2) * 2 * wide
+                        x, y = even[:, at : at + 2 * wide], odd[:, at : at + 2 * wide]
+                        if a % 2:
+                            x = pltpu.roll(x, wide, 1)
+                        else:
+                            y = pltpu.roll(y, wide, 1)
+                        blocks.append(jnp.where(lane_s < wide, x, y))
+                    peak = jnp.full((1, 2 * wide), 1e-30, F32)
+                    for block in blocks:
+                        peak = jnp.maximum(peak, jnp.max(jnp.abs(block), axis=0, keepdims=True))
+                    peak_out[quad, h] = peak
+                    scale = TOP / peak
+                    for a in range(nt):
+                        kept[quad, a, h] = blocks[a]
+                        sums_out[quad, a, h] = (
+                            jnp.floor(blocks[a] * scale + 0.5).astype(jnp.int32).astype(jnp.int16)
+                        )
 
                 @pl.loop(1, nt)
                 def _(d):
                     peer = lax.rem(tm + d, nt)
-                    remote(SUMS, sums_out.at[g, nt - 1 - peer], sums_in.at[tm, g], tm=peer).start()
-                    remote(PEAK, peak_out.at[g], peak_in.at[tm, g], tm=peer).start()
-
-    sums_in[tm] = jnp.zeros((groups, share, wide), jnp.int16)
-    peak_in[tm] = jnp.zeros((groups, 1, wide), F32)
+                    remote(SUMS, sums_out.at[quad, peer], sums_in.at[tm, quad], tm=peer).start()
+                    remote(PEAK, peak_out.at[quad], peak_in.at[tm, quad], tm=peer).start()
+
+    sums_in[tm] = jnp.zeros((quads, 2, share, 2 * wide), jnp.int16)
+    peak_in[tm] = jnp.zeros((quads, 2, 1, 2 * wide), F32)
     bytes_wait(sums_in.at[0 : nt - 1], rsem.at[SUMS])
     bytes_wait(peak_in.at[0 : nt - 1], rsem.at[PEAK])
 
     whole = []
-    for g in range(groups):
-        total = part[g, nt - 1 - tm]
-        for i in range(nt):
-            total += sums_in[i, g].astype(jnp.int32).astype(F32) * (peak_in[i, g] * (1.0 / TOP))
-        whole.append(total)
+    for quad in range(quads):
+        for h in range(2):
+            total = kept[quad, tm, h]
+            for i in range(nt):
+                total += sums_in[i, quad, h].astype(jnp.int32).astype(F32) * (peak_in[i, quad, h] * (1.0 / TOP))
+            whole.append(total)
     lag = tm * share + (share - 1) - iota((share, cells), 0)
     overlap = (valid_ref[...] - lag).astype(F32)
-    lane_o = iota((share, cells), 1)
-    each = cells // GROUP
+    place_o = iota((share, cells), 1) // GROUP
     for k in range(refs):
-        tile = k // each
         result = jnp.zeros((share, cells), F32)
         for g in range(groups):
-            piece = whole[g][:, tile * cells : (tile + 1) * cells]
-            shift = (GROUP * (g - k % each)) % cells
+            shift = (GROUP * g - wide * (g % 2) - GROUP * k) % cells
+            piece = whole[g // 2]
             if shift:
                 piece = pltpu.roll(piece, shift, 1)
-            result = jnp.where(lane_o // GROUP == g, piece, result)
+            result = jnp.where(place_o == g, piece, result)
         result = result / overlap
         for i in range(share):
             out_ref[share - 1 - i, k : k + 1, :] = result[i : i + 1]
@@ -339,6 +379,7 @@
         refs = rural_ids.shape[0]
         share = LAGS // nt
         groups, wide, slots, half = cells // GROUP, GROUP * refs, nc * CAP, nc // 2
+        quads = groups // 4
         span, rows = hours // PARTS, cells // CAP
         vmem = pl.BlockSpec(memory_space=pltpu.VMEM)
         whole = pl.BlockSpec(memory_space=pl.ANY)
@@ -361,12 +402,14 @@
                 pltpu.VMEM((2, half * CAP, cells), BF16),
                 pltpu.VMEM((PARTS, nc + 2 * rows, CAP, span), BF16),
                 pltpu.VMEM((cells * refs, slots + 2 * cells), BF16),
-                pltpu.VMEM((PARTS, cells, LAGS, span), BF16),
-                pltpu.VMEM((groups, nt, share, wide), F32),
-                pltpu.VMEM((groups, nt, share, wide), jnp.int16),
-                pltpu.VMEM((nt, groups, share, wide), jnp.int16),
-                pltpu.VMEM((groups, 1, wide), F32),
-                pltpu.VMEM((nt, groups, 1, wide), F32),
+                pltpu.VMEM((cells, share, hours + LAGS), BF16),
+                pltpu.VMEM((4, nt, wide, span + LAGS), BF16),
+                pltpu.VMEM((groups, share, nt * wide), F32),
+                pltpu.VMEM((quads, nt, 2, share, 2 * wide), F32),
+                pltpu.VMEM((quads, nt, 2, share, 2 * wide), jnp.int16),
+                pltpu.VMEM((nt, quads, 2, share, 2 * wide), jnp.int16),
+                pltpu.VMEM((quads, 2, 1, 2 * wide), F32),
+                pltpu.VMEM((nt, quads, 2, 1, 2 * wide), F32),
                 pltpu.SemaphoreType.DMA((2,)),
                 pltpu.SemaphoreType.DMA((KINDS,)),
                 pltpu.SemaphoreType.DMA((KINDS,)),

time: 48 us -> 46.9 us (0.977)
  Pallas kernels: 43.9 us -> 42.8 us
    pallas_call x1, Pallas kernels: 43.9 us -> 42.8 us  [shards(): pl.pallas_call(functools.partial(kernel, nc, nt), out_shape=jax.ShapeDtyp...]
where the time goes in v4:
time: 46.9 us; the launch traced here: 46.7 us
  Pallas kernels  42.8 us (91%)
  local copies, waits for them, and re-layouts  3.9 us (8%)
    pallas_call x1, Pallas kernels, shards(): pl.pallas_call(functools.partial(kernel, nc, nt), out_shape=jax.ShapeDtyp...  42.8 us
    unnamed x9, local copies, waits for them, and re-layouts  3.9 us

profile of v4, /device:TPU:1, one launch (start us, length us, event | category | flops | bytes accessed | tf_op | source)
XLA Modules:
  0.0 46.7 jit_solution(1247243946102311897)
XLA Ops:
  0.0 0.0 copy-start.3
  0.0 0.7 %copy-done.3 = s32[128]{0:T(128)S(1)} copy-done((s32[128]{0:T(128)S(1)}, s32[128]{0:T(128)}, u32[]{:S(2)}) %copy-start.3) | copy-done | bytes 536
  0.7 0.0 copy-start
  0.7 0.9 %copy-done = f32[512,128]{1,0:T(8,128)S(1)} copy-done((f32[512,128]{1,0:T(8,128)S(1)}, f32[512,128]{1,0:T(8,128)}, u32[]{:S(2)}) %copy-start) | copy-done | bytes 262168
  1.6 0.0 copy-start.1
  1.6 0.9 %copy-done.1 = f32[512,128]{1,0:T(8,128)S(1)} copy-done((f32[512,128]{1,0:T(8,128)S(1)}, f32[512,128]{1,0:T(8,128)}, u32[]{:S(2)}) %copy-start.1) | copy-done | bytes 262168
  2.6 0.0 copy-start.2
  2.6 0.7 %copy-done.2 = s32[8,128]{1,0:T(8,128)S(1)} copy-done((s32[8,128]{1,0:T(8,128)S(1)}, s32[8,128]{1,0:T(8,128)}, u32[]{:S(2)}) %copy-start.2) | copy-done | bytes 4120
  3.2 42.8 %shard_map.46 = f32[32,8,128]{2,1,0:T(8,128)S(1)} custom-call(f32[512,128]{1,0:T(8,128)S(1)} %copy-done, f32[512,128]{1,0:T(8,128)S(1)} %copy-done.1, s32[1,128]{1,0:T(1,128)S(1)} %bitcast.1, s32[8,128]{1,0:T(8,128)S(1)} %copy-done.2), custom_call_target="tpu_custom_call" | custom-call | tf_op jit(solution)/shard_map/pallas_call | solution.py:386
  46.1 0.7 %copy.6 = f32[32,8,128]{2,1,0:T(8,128)} copy(f32[32,8,128]{2,1,0:T(8,128)S(1)} %shard_map.46) | data formatting | bytes 262144
Async XLA Ops:
  0.0 0.7 %copy-start.3 = (s32[128]{0:T(128)S(1)}, s32[128]{0:T(128)}, u32[]{:S(2)}) copy-start(s32[128]{0:T(128)} %param.6) | copy-start | bytes 1540
  0.7 0.9 %copy-start = (f32[512,128]{1,0:T(8,128)S(1)}, f32[512,128]{1,0:T(8,128)}, u32[]{:S(2)}) copy-start(f32[512,128]{1,0:T(8,128)} %urban_hbm.1) | copy-start | bytes 786436
  1.6 0.9 %copy-start.1 = (f32[512,128]{1,0:T(8,128)S(1)}, f32[512,128]{1,0:T(8,128)}, u32[]{:S(2)}) copy-start(f32[512,128]{1,0:T(8,128)} %rural_hbm.1) | copy-start | bytes 786436
  2.6 0.7 %copy-start.2 = (s32[8,128]{1,0:T(8,128)S(1)}, s32[8,128]{1,0:T(8,128)}, u32[]{:S(2)}) copy-start(s32[8,128]{1,0:T(8,128)} %ids_ref.1) | copy-start | bytes 12292

commit v5 on v4

--- a/solution.py
+++ b/solution.py
@@ -162,22 +162,13 @@
         spread = second / n - average * average
         return (series - average) * lax.rsqrt(spread + EPSILON) * keep
 
-    rural_z = finish(rural_ref[...], total[2:3], total[3:4], F32(hours * nt), F32(1.0))
     for p in range(PARTS):
-        turned = jnp.transpose(rural_z[p * span : (p + 1) * span]).astype(BF16)
+        rural_z = finish(rural_ref[p * span : (p + 1) * span], total[2:3], total[3:4], F32(hours * nt), F32(1.0))
+        turned = jnp.transpose(rural_z).astype(BF16)
         fetched[p, nc : nc + rows] = turned.reshape(rows, CAP, span)
         remote(
             TWIN + p, fetched.at[p, nc : nc + rows], fetched.at[p, nc + rows : nc + 2 * rows], cells=twin
         ).start()
-    urban_z = finish(urban_ref[...], total[0:1], total[1:2], valid, mask)
-    for j in range(hours // LAGS):
-        ut[j] = jnp.transpose(urban_z[j * LAGS : (j + 1) * LAGS])
-    halo_out[...] = ut[0].astype(BF16)
-
-    @pl.when(tm > 0)
-    def _():
-        remote(HALO, halo_out, halo_in, tm=tm - 1).start()
-
     bytes_wait(req_in.at[0 : half - 1], rsem.at[REQ])
     batch = min(8, half)
     chunks = half // batch
@@ -221,17 +212,14 @@
             choose[rel, pl.ds(begin, height), :] = jnp.where(column == lane_h, 1.0, 0.0).astype(BF16)
         respond(0, 0, q)
 
-    for p in range(1, PARTS):
-        respond_all(0, p)
-
-    @pl.when(tm < nt - 1)
+    urban_z = finish(urban_ref[...], total[0:1], total[1:2], valid, mask)
+    for j in range(hours // LAGS):
+        ut[j] = jnp.transpose(urban_z[j * LAGS : (j + 1) * LAGS])
+    halo_out[...] = ut[0].astype(BF16)
+
+    @pl.when(tm > 0)
     def _():
-        bytes_wait(halo_in, rsem.at[HALO])
-        ut[hours // LAGS] = halo_in[...].astype(F32)
-
-    @pl.when(tm == nt - 1)
-    def _():
-        ut[hours // LAGS] = jnp.zeros((cells, LAGS), F32)
+        remote(HALO, halo_out, halo_in, tm=tm - 1).start()
 
     tiles = hours // LAGS
     lane8 = iota((8, LAGS), 1)
@@ -253,14 +241,21 @@
                     both = jnp.concatenate([halves[0][j], halves[1][j]], axis=0).astype(BF16)
                     toep[c, 16 * pair : 16 * pair + 16, j * LAGS : (j + 1) * LAGS] = both
 
-    step = cells // (2 * PARTS)
-    for p in range(PARTS):
-        build(p * step, (p + 1) * step)
-        bytes_wait(fetched.at[p, nc + rows : nc + 2 * rows], rsem.at[TWIN + p])
-        respond_all(1, p)
-
-    build(cells // 2, cells)
-
+    bytes_wait(fetched.at[0, nc + rows : nc + 2 * rows], rsem.at[TWIN + 0])
+    respond_all(1, 0)
+    respond_all(0, 1)
+    bytes_wait(fetched.at[1, nc + rows : nc + 2 * rows], rsem.at[TWIN + 1])
+    respond_all(1, 1)
+    @pl.when(tm < nt - 1)
+    def _():
+        bytes_wait(halo_in, rsem.at[HALO])
+        ut[hours // LAGS] = halo_in[...].astype(F32)
+
+    @pl.when(tm == nt - 1)
+    def _():
+        ut[hours // LAGS] = jnp.zeros((cells, LAGS), F32)
+
+    build(0, cells)
     column_of = lax.rem(iota((share, nt * wide), 1), GROUP)
     lane_t = iota((4 * wide, LAGS), 1)
     lane_s = iota((share, 2 * wide), 1)

time: 46.9 us -> 45.2 us (0.964)
  Pallas kernels: 42.8 us -> 41.1 us
    pallas_call x1, Pallas kernels: 42.8 us -> 41.1 us  [shards(): pl.pallas_call(functools.partial(kernel, nc, nt), out_shape=jax.ShapeDtyp...]
where the time goes in v5:
time: 45.2 us; the launch traced here: 45 us
  Pallas kernels  41.1 us (91%)
  local copies, waits for them, and re-layouts  3.9 us (9%)
    pallas_call x1, Pallas kernels, shards(): pl.pallas_call(functools.partial(kernel, nc, nt), out_shape=jax.ShapeDtyp...  41.1 us
    unnamed x9, local copies, waits for them, and re-layouts  3.9 us

profile of v5, /device:TPU:1, one launch (start us, length us, event | category | flops | bytes accessed | tf_op | source)
XLA Modules:
  0.0 45.0 jit_solution(10956093309268513360)
XLA Ops:
  0.0 0.0 copy-start.3
  0.0 0.7 %copy-done.3 = s32[128]{0:T(128)S(1)} copy-done((s32[128]{0:T(128)S(1)}, s32[128]{0:T(128)}, u32[]{:S(2)}) %copy-start.3) | copy-done | bytes 536
  0.7 0.0 copy-start
  0.7 0.9 %copy-done = f32[512,128]{1,0:T(8,128)S(1)} copy-done((f32[512,128]{1,0:T(8,128)S(1)}, f32[512,128]{1,0:T(8,128)}, u32[]{:S(2)}) %copy-start) | copy-done | bytes 262168
  1.6 0.0 copy-start.1
  1.6 0.9 %copy-done.1 = f32[512,128]{1,0:T(8,128)S(1)} copy-done((f32[512,128]{1,0:T(8,128)S(1)}, f32[512,128]{1,0:T(8,128)}, u32[]{:S(2)}) %copy-start.1) | copy-done | bytes 262168
  2.6 0.0 copy-start.2
  2.6 0.7 %copy-done.2 = s32[8,128]{1,0:T(8,128)S(1)} copy-done((s32[8,128]{1,0:T(8,128)S(1)}, s32[8,128]{1,0:T(8,128)}, u32[]{:S(2)}) %copy-start.2) | copy-done | bytes 4120
  3.2 41.1 %shard_map.46 = f32[32,8,128]{2,1,0:T(8,128)S(1)} custom-call(f32[512,128]{1,0:T(8,128)S(1)} %copy-done, f32[512,128]{1,0:T(8,128)S(1)} %copy-done.1, s32[1,128]{1,0:T(1,128)S(1)} %bitcast.1, s32[8,128]{1,0:T(8,128)S(1)} %copy-done.2), custom_call_target="tpu_custom_call" | custom-call | tf_op jit(solution)/shard_map/pallas_call | solution.py:381
  44.3 0.7 %copy.6 = f32[32,8,128]{2,1,0:T(8,128)} copy(f32[32,8,128]{2,1,0:T(8,128)S(1)} %shard_map.46) | data formatting | bytes 262144
Async XLA Ops:
  0.0 0.7 %copy-start.3 = (s32[128]{0:T(128)S(1)}, s32[128]{0:T(128)}, u32[]{:S(2)}) copy-start(s32[128]{0:T(128)} %param.6) | copy-start | bytes 1540
  0.7 0.9 %copy-start = (f32[512,128]{1,0:T(8,128)S(1)}, f32[512,128]{1,0:T(8,128)}, u32[]{:S(2)}) copy-start(f32[512,128]{1,0:T(8,128)} %urban_hbm.1) | copy-start | bytes 786436
  1.6 0.9 %copy-start.1 = (f32[512,128]{1,0:T(8,128)S(1)}, f32[512,128]{1,0:T(8,128)}, u32[]{:S(2)}) copy-start(f32[512,128]{1,0:T(8,128)} %rural_hbm.1) | copy-start | bytes 786436
  2.6 0.7 %copy-start.2 = (s32[8,128]{1,0:T(8,128)S(1)}, s32[8,128]{1,0:T(8,128)}, u32[]{:S(2)}) copy-start(s32[8,128]{1,0:T(8,128)} %ids_ref.1) | copy-start | bytes 12292

commit v6 on v5

--- a/solution.py
+++ b/solution.py
@@ -263,67 +263,67 @@
     for p in range(PARTS):
         bytes_wait(fetched.at[p, 0 : nc - 2], rsem.at[FETCH + p])
 
-        @pl.loop(0, quads)
-        def _(quad):
-            begin = pl.multiple_of(quad * 4 * wide, 4 * wide)
-            chosen = jnp.dot(
-                pick[pl.ds(begin, 4 * wide), :],
-                fetched[p].reshape(slots + 2 * cells, span),
-                preferred_element_type=F32,
-            )
-            pieces = [chosen[:, j * LAGS : (j + 1) * LAGS] for j in range(span // LAGS)]
-            none = jnp.zeros((4 * wide, LAGS), F32)
-            for a in range(nt):
-                shift = share * a
-                turned = [none] + [pltpu.roll(x, shift, 1) if a else x for x in pieces] + [none]
-                for j in range(span // LAGS + 1):
-                    piece = jnp.where(lane_t >= shift, turned[j + 1], turned[j]) if a else turned[j + 1]
-                    piece = piece.astype(BF16)
-                    for i in range(4):
-                        moved[i, a, :, j * LAGS : (j + 1) * LAGS] = piece[i * wide : (i + 1) * wide]
-            totals = []
-            for i in range(4):
-                g = 4 * quad + i
-                left = toep[pl.ds(GROUP * g, GROUP), :, p * span : p * span + reach].reshape(GROUP * share, reach)
-                sums = lax.dot_general(
-                    left, moved[i].reshape(nt * wide, reach), (((1,), (1,)), ((), ())), preferred_element_type=F32
+        for lot in ([range(quads)] if p < PARTS - 1 else [range(0, 2), range(2, quads)]):
+            for quad in lot:
+                begin = quad * 4 * wide
+                chosen = jnp.dot(
+                    pick[begin : begin + 4 * wide, :],
+                    fetched[p].reshape(slots + 2 * cells, span),
+                    preferred_element_type=F32,
                 )
-                total = sums[0:share]
-                for c in range(1, GROUP):
-                    total = jnp.where(column_of == c, sums[c * share : (c + 1) * share], total)
-                if p:
-                    total += part[g]
-                if p < PARTS - 1:
-                    part[g] = total
-                totals.append(total)
-            if p == PARTS - 1:
-                for h in range(2):
-                    even, odd = totals[2 * h], totals[2 * h + 1]
-                    blocks = []
-                    for a in range(nt):
-                        at = (a // 2) * 2 * wide
-                        x, y = even[:, at : at + 2 * wide], odd[:, at : at + 2 * wide]
-                        if a % 2:
-                            x = pltpu.roll(x, wide, 1)
-                        else:
-                            y = pltpu.roll(y, wide, 1)
-                        blocks.append(jnp.where(lane_s < wide, x, y))
-                    peak = jnp.full((1, 2 * wide), 1e-30, F32)
-                    for block in blocks:
-                        peak = jnp.maximum(peak, jnp.max(jnp.abs(block), axis=0, keepdims=True))
-                    peak_out[quad, h] = peak
-                    scale = TOP / peak
-                    for a in range(nt):
-                        kept[quad, a, h] = blocks[a]
-                        sums_out[quad, a, h] = (
-                            jnp.floor(blocks[a] * scale + 0.5).astype(jnp.int32).astype(jnp.int16)
-                        )
-
-                @pl.loop(1, nt)
-                def _(d):
-                    peer = lax.rem(tm + d, nt)
-                    remote(SUMS, sums_out.at[quad, peer], sums_in.at[tm, quad], tm=peer).start()
-                    remote(PEAK, peak_out.at[quad], peak_in.at[tm, quad], tm=peer).start()
+                pieces = [chosen[:, j * LAGS : (j + 1) * LAGS] for j in range(span // LAGS)]
+                none = jnp.zeros((4 * wide, LAGS), F32)
+                for a in range(nt):
+                    shift = share * a
+                    turned = [none] + [pltpu.roll(x, shift, 1) if a else x for x in pieces] + [none]
+                    for j in range(span // LAGS + 1):
+                        piece = jnp.where(lane_t >= shift, turned[j + 1], turned[j]) if a else turned[j + 1]
+                        piece = piece.astype(BF16)
+                        for i in range(4):
+                            moved[quad, i, a, :, j * LAGS : (j + 1) * LAGS] = piece[i * wide : (i + 1) * wide]
+            for quad in lot:
+                totals = []
+                for i in range(4):
+                    g = 4 * quad + i
+                    left = toep[GROUP * g : GROUP * (g + 1), :, p * span : p * span + reach].reshape(GROUP * share, reach)
+                    sums = lax.dot_general(
+                        left, moved[quad, i].reshape(nt * wide, reach), (((1,), (1,)), ((), ())), preferred_element_type=F32
+                    )
+                    total = sums[0:share]
+                    for c in range(1, GROUP):
+                        total = jnp.where(column_of == c, sums[c * share : (c + 1) * share], total)
+                    if p:
+                        total += part[g]
+                    if p < PARTS - 1:
+                        part[g] = total
+                    totals.append(total)
+                if p == PARTS - 1:
+                    for h in range(2):
+                        even, odd = totals[2 * h], totals[2 * h + 1]
+                        blocks = []
+                        for a in range(nt):
+                            at = (a // 2) * 2 * wide
+                            x, y = even[:, at : at + 2 * wide], odd[:, at : at + 2 * wide]
+                            if a % 2:
+                                x = pltpu.roll(x, wide, 1)
+                            else:
+                                y = pltpu.roll(y, wide, 1)
+                            blocks.append(jnp.where(lane_s < wide, x, y))
+                        peak = jnp.full((1, 2 * wide), 1e-30, F32)
+                        for block in blocks:
+                            peak = jnp.maximum(peak, jnp.max(jnp.abs(block), axis=0, keepdims=True))
+                        peak_out[quad, h] = peak
+                        scale = TOP / peak
+                        for a in range(nt):
+                            kept[quad, a, h] = blocks[a]
+                            sums_out[quad, a, h] = (
+                                jnp.floor(blocks[a] * scale + 0.5).astype(jnp.int32).astype(jnp.int16)
+                            )
+
+                    for d in range(1, nt):
+                        peer = lax.rem(tm + d, nt)
+                        remote(SUMS, sums_out.at[quad, peer], sums_in.at[tm, quad], tm=peer).start()
+                        remote(PEAK, peak_out.at[quad], peak_in.at[tm, quad], tm=peer).start()
 
     sums_in[tm] = jnp.zeros((quads, 2, share, 2 * wide), jnp.int16)
     peak_in[tm] = jnp.zeros((quads, 2, 1, 2 * wide), F32)
@@ -398,7 +398,7 @@
                 pltpu.VMEM((PARTS, nc + 2 * rows, CAP, span), BF16),
                 pltpu.VMEM((cells * refs, slots + 2 * cells), BF16),
                 pltpu.VMEM((cells, share, hours + LAGS), BF16),
-                pltpu.VMEM((4, nt, wide, span + LAGS), BF16),
+                pltpu.VMEM((quads, 4, nt, wide, span + LAGS), BF16),
                 pltpu.VMEM((groups, share, nt * wide), F32),
                 pltpu.VMEM((quads, nt, 2, share, 2 * wide), F32),
                 pltpu.VMEM((quads, nt, 2, share, 2 * wide), jnp.int16),

time: 45.2 us -> 43.7 us (0.967)
  Pallas kernels: 41.1 us -> 39.6 us
    pallas_call x1, Pallas kernels: 41.1 us -> 39.6 us  [shards(): pl.pallas_call(functools.partial(kernel, nc, nt), out_shape=jax.ShapeDtyp...]
where the time goes in v6:
time: 43.7 us; the launch traced here: 43.6 us
  Pallas kernels  39.6 us (91%)
  local copies, waits for them, and re-layouts  3.9 us (9%)
    pallas_call x1, Pallas kernels, shards(): pl.pallas_call(functools.partial(kernel, nc, nt), out_shape=jax.ShapeDtyp...  39.6 us
    unnamed x9, local copies, waits for them, and re-layouts  3.9 us

profile of v6, /device:TPU:1, one launch (start us, length us, event | category | flops | bytes accessed | tf_op | source)
XLA Modules:
  0.0 43.6 jit_solution(8757705274130186540)
XLA Ops:
  0.0 0.0 copy-start.3
  0.0 0.7 %copy-done.3 = s32[128]{0:T(128)S(1)} copy-done((s32[128]{0:T(128)S(1)}, s32[128]{0:T(128)}, u32[]{:S(2)}) %copy-start.3) | copy-done | bytes 536
  0.7 0.0 copy-start
  0.7 0.9 %copy-done = f32[512,128]{1,0:T(8,128)S(1)} copy-done((f32[512,128]{1,0:T(8,128)S(1)}, f32[512,128]{1,0:T(8,128)}, u32[]{:S(2)}) %copy-start) | copy-done | bytes 262168
  1.6 0.0 copy-start.1
  1.6 0.9 %copy-done.1 = f32[512,128]{1,0:T(8,128)S(1)} copy-done((f32[512,128]{1,0:T(8,128)S(1)}, f32[512,128]{1,0:T(8,128)}, u32[]{:S(2)}) %copy-start.1) | copy-done | bytes 262168
  2.6 0.0 copy-start.2
  2.6 0.7 %copy-done.2 = s32[8,128]{1,0:T(8,128)S(1)} copy-done((s32[8,128]{1,0:T(8,128)S(1)}, s32[8,128]{1,0:T(8,128)}, u32[]{:S(2)}) %copy-start.2) | copy-done | bytes 4120
  3.2 39.6 %shard_map.46 = f32[32,8,128]{2,1,0:T(8,128)S(1)} custom-call(f32[512,128]{1,0:T(8,128)S(1)} %copy-done, f32[512,128]{1,0:T(8,128)S(1)} %copy-done.1, s32[1,128]{1,0:T(1,128)S(1)} %bitcast.1, s32[8,128]{1,0:T(8,128)S(1)} %copy-done.2), custom_call_target="tpu_custom_call" | custom-call | tf_op jit(solution)/shard_map/pallas_call | solution.py:381
  42.9 0.7 %copy.6 = f32[32,8,128]{2,1,0:T(8,128)} copy(f32[32,8,128]{2,1,0:T(8,128)S(1)} %shard_map.46) | data formatting | bytes 262144
Async XLA Ops:
  0.0 0.7 %copy-start.3 = (s32[128]{0:T(128)S(1)}, s32[128]{0:T(128)}, u32[]{:S(2)}) copy-start(s32[128]{0:T(128)} %param.6) | copy-start | bytes 1540
  0.7 0.9 %copy-start = (f32[512,128]{1,0:T(8,128)S(1)}, f32[512,128]{1,0:T(8,128)}, u32[]{:S(2)}) copy-start(f32[512,128]{1,0:T(8,128)} %urban_hbm.1) | copy-start | bytes 786436
  1.6 0.9 %copy-start.1 = (f32[512,128]{1,0:T(8,128)S(1)}, f32[512,128]{1,0:T(8,128)}, u32[]{:S(2)}) copy-start(f32[512,128]{1,0:T(8,128)} %rural_hbm.1) | copy-start | bytes 786436
  2.6 0.7 %copy-start.2 = (s32[8,128]{1,0:T(8,128)S(1)}, s32[8,128]{1,0:T(8,128)}, u32[]{:S(2)}) copy-start(s32[8,128]{1,0:T(8,128)} %ids_ref.1) | copy-start | bytes 12292

commit v7 on v6

--- a/solution.py
+++ b/solution.py
@@ -30,8 +30,8 @@
 
 
 def kernel(
-    nc, nt, urban_hbm, rural_hbm, valid_ref, ids_ref, out_ref,
-    urban_ref, rural_ref, req_out, req_in, slot_rows, stats, ut, halo_out, halo_in,
+    nc, nt, urban_hbm, rural_hbm, valid_hbm, ids_hbm, out_ref,
+    urban_ref, rural_ref, valid_ref, ids_ref, req_out, req_in, slot_rows, stats, ut, halo_out, halo_in,
     answer, choose, fetched, pick, toep, moved, part, kept, sums_out, sums_in, peak_out, peak_in, local_sem, ssem, rsem,
 ):
     hours, cells = urban_ref.shape
@@ -56,6 +56,12 @@
             device_id=where, device_id_type=MESH,
         )
 
+    pairs = ((ids_hbm, ids_ref), (valid_hbm, valid_ref), (rural_hbm, rural_ref), (urban_hbm, urban_ref))
+    copies = [pltpu.make_async_copy(src, dst, local_sem.at[i]) for i, (src, dst) in enumerate(pairs)]
+    ids_in, valid_in, rural_in, urban_in = copies
+    for copy in copies:
+        copy.start()
+
     barrier = pltpu.get_barrier_semaphore()
 
     @pl.loop(1, nt)
@@ -69,11 +75,7 @@
         peer = side * half + lax.rem(place + d, half)
         pl.semaphore_signal(barrier, inc=1, device_id={"cells": peer}, device_id_type=MESH)
 
-    rural_in = pltpu.make_async_copy(rural_hbm, rural_ref, local_sem.at[0])
-    urban_in = pltpu.make_async_copy(urban_hbm, urban_ref, local_sem.at[1])
-    rural_in.start()
-    urban_in.start()
-
+    ids_in.wait()
     ids = ids_ref[...]
     owner = (ids >> 7).astype(F32)
     local = (ids & 127).astype(F32)
@@ -106,6 +108,7 @@
     for q in range(half):
         req_out[q] = asks[2 * q : 2 * q + 2]
 
+    valid_in.wait()
     valid = valid_ref[...].astype(F32)
     hour = (tm * hours + iota((hours, cells), 0)).astype(F32)
     mask = (hour < valid).astype(F32)
@@ -162,13 +165,15 @@
         spread = second / n - average * average
         return (series - average) * lax.rsqrt(spread + EPSILON) * keep
 
-    for p in range(PARTS):
+    def settle(p):
         rural_z = finish(rural_ref[p * span : (p + 1) * span], total[2:3], total[3:4], F32(hours * nt), F32(1.0))
         turned = jnp.transpose(rural_z).astype(BF16)
         fetched[p, nc : nc + rows] = turned.reshape(rows, CAP, span)
         remote(
             TWIN + p, fetched.at[p, nc : nc + rows], fetched.at[p, nc + rows : nc + 2 * rows], cells=twin
         ).start()
+    settle(0)
+
     bytes_wait(req_in.at[0 : half - 1], rsem.at[REQ])
     batch = min(8, half)
     chunks = half // batch
@@ -199,18 +204,26 @@
         def _(step):
             respond(rel, p, lax.rem(place // batch + step, chunks))
 
+    def prepare(rel, q):
+        begin = pl.multiple_of(q * height, height)
+        columns = []
+        for s in range(batch):
+            asked = req_in[q * batch + s][rel : rel + 1].astype(F32)
+            columns.append(jnp.sum(jnp.where(here, asked, 0.0), axis=1, keepdims=True))
+        column = jnp.concatenate(columns, axis=0).astype(jnp.int32)
+        choose[rel, pl.ds(begin, height), :] = jnp.where(column == lane_h, 1.0, 0.0).astype(BF16)
+
     @pl.loop(0, chunks)
     def _(step):
         q = lax.rem(place // batch + step, chunks)
-        begin = pl.multiple_of(q * height, height)
-        for rel in range(2):
-            columns = []
-            for s in range(batch):
-                asked = req_in[q * batch + s][rel : rel + 1].astype(F32)
-                columns.append(jnp.sum(jnp.where(here, asked, 0.0), axis=1, keepdims=True))
-            column = jnp.concatenate(columns, axis=0).astype(jnp.int32)
-            choose[rel, pl.ds(begin, height), :] = jnp.where(column == lane_h, 1.0, 0.0).astype(BF16)
+        prepare(0, q)
         respond(0, 0, q)
+
+    for p in range(1, PARTS):
+        settle(p)
+    @pl.loop(0, chunks)
+    def _(q):
+        prepare(1, q)
 
     urban_z = finish(urban_ref[...], total[0:1], total[1:2], valid, mask)
     for j in range(hours // LAGS):
@@ -320,8 +333,8 @@
                                 jnp.floor(blocks[a] * scale + 0.5).astype(jnp.int32).astype(jnp.int16)
                             )
 
-                    for d in range(1, nt):
-                        peer = lax.rem(tm + d, nt)
+                    for d in list(range(nt // 2, nt)) + list(range(1, nt // 2)):
+                        peer = tm ^ d
                         remote(SUMS, sums_out.at[quad, peer], sums_in.at[tm, quad], tm=peer).start()
                         remote(PEAK, peak_out.at[quad], peak_in.at[tm, quad], tm=peer).start()
 
@@ -376,16 +389,16 @@
         groups, wide, slots, half = cells // GROUP, GROUP * refs, nc * CAP, nc // 2
         quads = groups // 4
         span, rows = hours // PARTS, cells // CAP
-        vmem = pl.BlockSpec(memory_space=pltpu.VMEM)
-        whole = pl.BlockSpec(memory_space=pl.ANY)
         return pl.pallas_call(
             functools.partial(kernel, nc, nt),
             out_shape=jax.ShapeDtypeStruct((share, refs, cells), F32),
-            in_specs=[whole, whole, vmem, vmem],
-            out_specs=vmem,
+            in_specs=[pl.BlockSpec(memory_space=pltpu.HBM)] * 4,
+            out_specs=pl.BlockSpec(memory_space=pltpu.VMEM),
             scratch_shapes=[
                 pltpu.VMEM((hours, cells), F32),
                 pltpu.VMEM((hours, cells), F32),
+                pltpu.VMEM((1, cells), jnp.int32),
+                pltpu.VMEM((refs, cells), jnp.int32),
                 pltpu.VMEM((half, 2, cells), jnp.int32),
                 pltpu.VMEM((half, 2, cells), jnp.int32),
                 pltpu.VMEM((refs, cells), F32),
@@ -405,12 +418,12 @@
                 pltpu.VMEM((nt, quads, 2, share, 2 * wide), jnp.int16),
                 pltpu.VMEM((quads, 2, 1, 2 * wide), F32),
                 pltpu.VMEM((nt, quads, 2, 1, 2 * wide), F32),
-                pltpu.SemaphoreType.DMA((2,)),
+                pltpu.SemaphoreType.DMA((4,)),
                 pltpu.SemaphoreType.DMA((KINDS,)),
                 pltpu.SemaphoreType.DMA((KINDS,)),
             ],
             compiler_params=pltpu.CompilerParams(
-                collective_id=0, has_side_effects=True, vmem_limit_bytes=52 * 1024 * 1024
+                collective_id=0, has_side_effects=True, vmem_limit_bytes=62 * 1024 * 1024
             ),
         )(urban, rural, urban_valid.reshape(1, cells), rural_ids)
 

time: 43.7 us -> 42 us (0.961)
  local copies, waits for them, and re-layouts: 3.9 us -> 1.57 us
  Pallas kernels: 39.6 us -> 40.3 us
    unnamed x9 -> x1, local copies, waits for them, and re-layouts: 3.9 us -> 1.57 us
    pallas_call x1, Pallas kernels: 39.6 us -> 40.3 us  [shards(): pl.pallas_call(functools.partial(kernel, nc, nt), out_shape=jax.ShapeDtyp...]
where the time goes in v7:
time: 42 us; the launch traced here: 41.9 us
  Pallas kernels  40.3 us (96%)
  local copies, waits for them, and re-layouts  1.57 us (4%)
    pallas_call x1, Pallas kernels, shards(): pl.pallas_call(functools.partial(kernel, nc, nt), out_shape=jax.ShapeDtyp...  40.3 us
    unnamed x1, local copies, waits for them, and re-layouts  1.57 us

profile of v7, /device:TPU:1, one launch (start us, length us, event | category | flops | bytes accessed | tf_op | source)
XLA Modules:
  0.0 41.9 jit_solution(15232077530935159898)
XLA Ops:
  0.0 40.3 %shard_map.46 = f32[32,8,128]{2,1,0:T(8,128)} custom-call(f32[512,128]{1,0:T(8,128)} %urban_hbm.1, f32[512,128]{1,0:T(8,128)} %rural_hbm.1, s32[1,128]{1,0:T(1,128)} %bitcast.1, s32[8,128]{1,0:T(8,128)} %ids_hbm.1), custom_call_target="tpu_custom_call" | custom-call | tf_op jit(solution)/shard_map/pallas_call | solution.py:392
  40.3 1.6 %copy.6 = f32[32,8,128]{2,1,0:T(8,128)} copy(f32[32,8,128]{2,1,0:T(8,128)} %shard_map.46) | data formatting | bytes 262144

commit v8 on v7

--- a/solution.py
+++ b/solution.py
@@ -276,7 +276,7 @@
     for p in range(PARTS):
         bytes_wait(fetched.at[p, 0 : nc - 2], rsem.at[FETCH + p])
 
-        for lot in ([range(quads)] if p < PARTS - 1 else [range(0, 2), range(2, quads)]):
+        for lot in ([range(quads)] if p < PARTS - 1 else [[q] for q in range(quads)]):
             for quad in lot:
                 begin = quad * 4 * wide
                 chosen = jnp.dot(

time: 42 us -> 41.7 us (level)
  no operation moved by 1% of the time
where the time goes in v8:
time: 41.7 us; the launch traced here: 41.6 us
  Pallas kernels  40 us (96%)
  local copies, waits for them, and re-layouts  1.57 us (4%)
    pallas_call x1, Pallas kernels, shards(): pl.pallas_call(functools.partial(kernel, nc, nt), out_shape=jax.ShapeDtyp...  40 us
    unnamed x1, local copies, waits for them, and re-layouts  1.57 us

profile of v8, /device:TPU:1, one launch (start us, length us, event | category | flops | bytes accessed | tf_op | source)
XLA Modules:
  0.0 41.6 jit_solution(11609602501758450236)
XLA Ops:
  0.0 40.0 %shard_map.46 = f32[32,8,128]{2,1,0:T(8,128)} custom-call(f32[512,128]{1,0:T(8,128)} %urban_hbm.1, f32[512,128]{1,0:T(8,128)} %rural_hbm.1, s32[1,128]{1,0:T(1,128)} %bitcast.1, s32[8,128]{1,0:T(8,128)} %ids_hbm.1), custom_call_target="tpu_custom_call" | custom-call | tf_op jit(solution)/shard_map/pallas_call | solution.py:392
  40.0 1.6 %copy.6 = f32[32,8,128]{2,1,0:T(8,128)} copy(f32[32,8,128]{2,1,0:T(8,128)} %shard_map.46) | data formatting | bytes 262144
